TPU v7x, 32 devices: a whole 2x2x4 slice. The times are simulated.
32 devices in a mesh: panel: 2 (over core), ang: 4 (over z), rad: 4 (over y, x).
Axes of the slice: x: 2, y: 2, z: 4, core: 2. Of those that a mesh axis runs over, the one named last changes fastest.
Arguments:
- density: float32 [2, 8, 64, 512], P('panel', 'rad', 'ang'), may hold values from 1 to 2
- momentum: float32 [2, 3, 8, 64, 512], P('panel', None, 'rad', 'ang'), may hold values from -2.5 to 2.5
- magnetic: float32 [2, 3, 8, 64, 512], P('panel', None, 'rad', 'ang'), may hold values from -2.5 to 2.5
- partner_device: int32 [2, 128, 1], P('panel', 'ang'), may hold values from 0 to 3; in each aligned block of 32 rows (0 to 31, 32 to 63, ..., all dimensions but the last counted through in order) at most 16 rows name the same one
- partner_phi: int32 [2, 128], P('panel', 'ang'), may hold values from 0 to 14
- partner_theta: int32 [2, 128], P('panel', 'ang'), may hold values from 0 to 510
- partner_weight: float32 [2, 128, 4], P('panel', 'ang'), may hold values from 0 to 1, as said below
- border_turn: float32 [2, 128], P('panel', 'ang'), may hold values from -3.140625 to 3.140625
Outputs:
- density_next: float32 [2, 8, 64, 512], P('panel', 'rad', 'ang')
- momentum_next: float32 [2, 3, 8, 64, 512], P('panel', None, 'rad', 'ang')
- magnetic_next: float32 [2, 3, 8, 64, 512], P('panel', None, 'rad', 'ang')
Inputs may be any that keep to these rules, and one draw needn't show every extreme that they name: `partner_device`: within the 32 table rows of one device (aligned blocks), at most 16 rows name the same source device. `partner_weight`: each row's weights are (1-u)(1-v), (1-u)v, u(1-v), uv for some u, v in [0, 1].
All inputs are finite; a program needn't handle non-finite values.
Results may differ from a plain program's by a relative error of at most 0.00005.
Values sent between devices are 32-bit elements; how exact they have to be, the bound alone decides.
A program may use at most 64 MiB of HBM per device.

v0:
```python
import math

import jax
import jax.numpy as jnp
from jax import lax
from jax.sharding import PartitionSpec as P

time_step = 0.15
sound_sq = 1.0
viscosity = 0.1
resistivity = 0.1
r_inner = 0.35


def padded(value, sides, width):
    for axis, dim in sides:
        size, length = (lax.axis_size(axis), value.shape[dim])
        up = [(i, (i + 1) % size) for i in range(size - 1)]
        down = [(j, i) for i, j in up]
        last = lax.slice_in_dim(value, length - width, length, axis=dim)
        first = lax.slice_in_dim(value, 0, width, axis=dim)
        before = lax.ppermute(last, axis, up)
        after = lax.ppermute(first, axis, down)
        value = jnp.concatenate([before, value, after], axis=dim)
    return value


def field_of(block, index):
    return block[..., index, :, :, :]


def fluxes(block, direction):
    mass_field = field_of(block, 0)
    moment = [field_of(block, 1 + component) for component in range(3)]
    magnet = [field_of(block, 4 + component) for component in range(3)]
    velocity = [moment[component] / mass_field for component in range(3)]
    pressure = sound_sq * mass_field + 0.5 * (
        magnet[0] * magnet[0] + magnet[1] * magnet[1] + magnet[2] * magnet[2]
    )
    pieces = [moment[direction]]
    for component in range(3):
        flux_term = moment[component] * velocity[direction] - magnet[component] * magnet[direction]
        if component == direction:
            flux_term = flux_term + pressure
        pieces.append(flux_term)
    for component in range(3):
        pieces.append(
            velocity[direction] * magnet[component] - magnet[direction] * velocity[component]
        )
    return jnp.stack(pieces, axis=-4)


def tendency(current, radial, polar, azimuth, half_t, half_p, sq_t, sq_p):
    flux_r = fluxes(radial, 0)
    flux_t = fluxes(polar, 1)
    flux_p = fluxes(azimuth, 2)
    divergence = (flux_r[..., 2:, :, :] - flux_r[..., :-2, :, :]) * 0.5
    divergence = divergence + (flux_t[..., 2:] - flux_t[..., :-2]) * half_t
    divergence = divergence + (flux_p[..., :, 2:, :] - flux_p[..., :, :-2, :]) * half_p
    laplace_sum = radial[..., 2:, :, :] - 2.0 * current + radial[..., :-2, :, :]
    laplace_sum = laplace_sum + (polar[..., 2:] - 2.0 * current + polar[..., :-2]) * sq_t
    laplace_sum = (
        laplace_sum + (azimuth[..., :, 2:, :] - 2.0 * current + azimuth[..., :, :-2, :]) * sq_p
    )
    mixing = jnp.array(
        [0.0, viscosity, viscosity, viscosity, resistivity, resistivity, resistivity], jnp.float32
    ).reshape(7, 1, 1, 1)
    return mixing * laplace_sum - divergence


def turn_frame(ghost, cosine, sine):
    pieces = [ghost[0], ghost[1]]
    pieces.append(cosine * ghost[2] + sine * ghost[3])
    pieces.append(cosine * ghost[3] - sine * ghost[2])
    pieces.append(ghost[4])
    pieces.append(cosine * ghost[5] + sine * ghost[6])
    pieces.append(cosine * ghost[6] - sine * ghost[5])
    return jnp.stack(pieces, axis=0)


def route_request(packed):
    panel_side = lax.axis_index("panel")
    zeroed = jnp.zeros_like(packed)
    doubled = jnp.where(
        panel_side == 0,
        jnp.concatenate([zeroed, packed], axis=0),
        jnp.concatenate([packed, zeroed], axis=0),
    )
    received = lax.all_to_all(doubled, ("panel", "ang"), split_axis=0, concat_axis=0, tiled=True)
    return lax.dynamic_slice_in_dim(
        received, (1 - panel_side) * packed.shape[0], packed.shape[0], 0
    )


def route_reply(answer):
    panel_side = lax.axis_index("panel")
    zeroed = jnp.zeros_like(answer)
    doubled = jnp.where(
        panel_side == 0,
        jnp.concatenate([zeroed, answer], axis=1),
        jnp.concatenate([answer, zeroed], axis=1),
    )
    received = lax.all_to_all(doubled, ("panel", "ang"), split_axis=1, concat_axis=1, tiled=True)
    return lax.dynamic_slice_in_dim(
        received, (1 - panel_side) * answer.shape[1], answer.shape[1], 1
    )


def body(
    density,
    momentum,
    magnetic,
    partner_device,
    partner_phi,
    partner_theta,
    partner_weight,
    border_turn,
):
    fields_now = jnp.concatenate([density, momentum[0], magnetic[0]], axis=0)
    fields, rows_r, rows_p, rows_t = fields_now.shape
    n_ang = lax.axis_size("ang")
    n_rad = lax.axis_size("rad")
    border = partner_phi.shape[1]
    capacity = max(2, 2 * border // n_ang)
    slot_count = n_ang * capacity
    stacked_rows = fields * rows_r
    highest = lax.Precision.HIGHEST
    level = lax.axis_index("rad") * rows_r + jnp.arange(rows_r, dtype=jnp.int32)
    radius = r_inner + (level.astype(jnp.float32) + 0.5) * ((1.0 - r_inner) / (rows_r * n_rad))
    colatitude = math.pi / 4 + (jnp.arange(rows_t).astype(jnp.float32) + 0.5) * (
        math.pi / 2 / rows_t
    )
    inv_radius = (1.0 / radius).reshape(rows_r, 1, 1)
    inv_both = inv_radius / jnp.sin(colatitude)
    half_t = 0.5 * inv_radius
    half_p = 0.5 * inv_both
    sq_t = inv_radius * inv_radius
    sq_p = inv_both * inv_both
    mirror = jnp.array([1.0, -1.0, -1.0, -1.0, 1.0, 1.0, 1.0], jnp.float32).reshape(7, 1, 1, 1)
    first_r = lax.axis_index("rad") == 0
    last_r = lax.axis_index("rad") == n_rad - 1
    first_p = lax.axis_index("ang") == 0
    last_p = lax.axis_index("ang") == n_ang - 1
    source_ang = partner_device[0, :, 0]
    one_hot = (source_ang[:, None] == jnp.arange(n_ang, dtype=jnp.int32)[None, :]).astype(jnp.int32)
    ranked = jnp.sum(one_hot * (jnp.cumsum(one_hot, axis=0) - 1), axis=1)
    target_slot = source_ang * capacity + ranked
    placing = (jnp.arange(slot_count, dtype=jnp.int32)[:, None] == target_slot[None, :]).astype(
        jnp.float32
    )
    base_cell = (partner_phi[0] * rows_t + partner_theta[0]).astype(jnp.float32)
    weights = partner_weight[0]
    payload = base_cell[:, None]
    packed = jnp.dot(placing, payload, precision=highest).reshape(n_ang, capacity, payload.shape[1])
    asked = route_request(packed)
    cell_index = (asked[:, :, 0].reshape(slot_count) + 0.5).astype(jnp.int32)
    offsets = jnp.array([0, 1, rows_t, rows_t + 1], jnp.int32)
    gather_index = (cell_index[:, None] + offsets[None, :]).reshape(slot_count * 4)
    cosine = jnp.cos(border_turn[0])
    sine = jnp.sin(border_turn[0])

    def overset(current):
        table = current.reshape(stacked_rows, rows_p * rows_t)
        corner = jnp.take(table, gather_index, axis=1).reshape(stacked_rows, slot_count, 4)
        returned = route_reply(corner.reshape(stacked_rows, n_ang, capacity, 4)).reshape(
            stacked_rows, slot_count, 4
        )
        picked = [jnp.dot(returned[:, :, index], placing, precision=highest) for index in range(4)]
        ghost = weights[:, 0] * picked[0] + weights[:, 1] * picked[1]
        ghost = ghost + weights[:, 2] * picked[2]
        ghost = ghost + weights[:, 3] * picked[3]
        ghost = turn_frame(ghost.reshape(fields, rows_r, border), cosine, sine)
        return (ghost[:, :, :rows_p], ghost[:, :, rows_p:])

    def evaluate(current):
        haloed = padded(current, (("ang", 2), ("rad", 1)), 1)
        lower_r = jnp.where(first_r, mirror * current[:, :1], haloed[:, :1, 1:-1])
        upper_r = jnp.where(last_r, mirror * current[:, -1:], haloed[:, -1:, 1:-1])
        lower_p = jnp.where(first_p, mirror * current[:, :, :1], haloed[:, 1:-1, :1])
        upper_p = jnp.where(last_p, mirror * current[:, :, -1:], haloed[:, 1:-1, -1:])
        radial = jnp.concatenate([lower_r, current, upper_r], axis=1)
        azimuth = jnp.concatenate([lower_p, current, upper_p], axis=2)
        lower_t, upper_t = overset(current)
        polar = jnp.concatenate([lower_t[..., None], current, upper_t[..., None]], axis=3)
        return tendency(current, radial, polar, azimuth, half_t, half_p, sq_t, sq_p)

    slope_one = evaluate(fields_now)
    slope_two = evaluate(fields_now + 0.5 * time_step * slope_one)
    slope_three = evaluate(fields_now + 0.5 * time_step * slope_two)
    slope_four = evaluate(fields_now + time_step * slope_three)
    updated = fields_now + time_step / 6.0 * (
        slope_one + 2.0 * slope_two + 2.0 * slope_three + slope_four
    )
    return (updated[0:1], updated[1:4][None], updated[4:7][None])


def solution(mesh):
    in_specs = (
        P("panel", "rad", "ang", None),
        P("panel", None, "rad", "ang", None),
        P("panel", None, "rad", "ang", None),
        P("panel", "ang", None),
        P("panel", "ang"),
        P("panel", "ang"),
        P("panel", "ang", None),
        P("panel", "ang"),
    )
    out_specs = (
        P("panel", "rad", "ang", None),
        P("panel", None, "rad", "ang", None),
        P("panel", None, "rad", "ang", None),
    )
    return jax.shard_map(body, mesh=mesh, in_specs=in_specs, out_specs=out_specs, check_vma=False)
```

profile of v0, /device:TPU:0, one launch (start us, length us, event | category | flops | bytes accessed | tf_op | source)
XLA Modules:
  0.0 177.4 jit_solution(17220008848022054274)
XLA Ops:
  3.1 5.6 %collective-permute-start = (f32[7,2,1,512]{3,2,1,0:T(1,128)S(1)}, f32[7,2,1,512]{3,2,1,0:T(1,128)S(1)}, u32[]{:S(2)}, u32[]{:S(2)}) collective-permute-start(f32[7,2,1,512]{3,2,1,0:T(1,128)S(1)} %get-tuple-element.74), channel_id=1, source_target_pairs={{0,4},{4,8},{8,12},{1,5},{5,9},{9,13},{2,6},{6,10},{10,14},{3,7},{... | collective-permute-start | bytes 86024 | tf_op jit(solution)/shard_map/ppermute | solution.py:22
  12.5 4.3 %all-to-all-start = ((f32[8,16,1]{1,2,0:T(1,128)}), f32[8,16,1]{1,2,0:T(1,128)S(1)}, u32[]{:S(2)}, u32[]{:S(2)}) async-start(f32[8,16,1]{1,2,0:T(1,128)} %bitcast.10), calls=%async_computation | async-start | bytes 8192 | tf_op jit(solution)/shard_map/all_to_all | solution.py:89
  22.7 2.9 %gather_fusion = f32[256,14]{1,0:T(8,128)S(1)} fusion(f32[14,8192]{0,1:T(8,128)} %copy.87, s32[1024]{0:T(1024)S(1)} %pad_clamp_fusion), kind=kCustom, calls=%fused_computation.clone | custom fusion | bytes 29696 | tf_op jit(solution)/shard_map/jit(_take)/gather | solution.py:164
  26.7 4.4 %all-to-all-start.1 = ((f32[8,1,896]{2,1,0:T(1,128)}), f32[8,1,896]{2,1,0:T(1,128)S(1)}, u32[]{:S(2)}, u32[]{:S(2)}) async-start(f32[8,1,896]{2,1,0:T(1,128)} %reshape.315), calls=%async_computation.1 | async-start | bytes 57344 | tf_op jit(solution)/shard_map/all_to_all | solution.py:103
  32.6 4.1 %collective-permute-start.3 = (f32[7,1,18,512]{3,2,1,0:T(8,128)}, f32[7,1,18,512]{3,2,1,0:T(8,128)}, u32[]{:S(2)}, u32[]{:S(2)}) collective-permute-start(f32[7,1,18,512]{3,2,1,0:T(8,128)} %get-tuple-element.40), channel_id=1, source_target_pairs={{0,1},{1,2},{2,3},{4,5},{5,6},{6,7},{8,9},{9,10},{10,11},{12,13},{... | collective-permute-start | bytes 774152 | tf_op jit(solution)/shard_map/ppermute | solution.py:22
  41.2 3.1 %collective-permute-done.3 = f32[7,1,18,512]{3,2,1,0:T(8,128)} collective-permute-done((f32[7,1,18,512]{3,2,1,0:T(8,128)}, f32[7,1,18,512]{3,2,1,0:T(8,128)}, u32[]{:S(2)}, u32[]{:S(2)}) %collective-permute-start.3) | collective-permute-done | bytes 258080 | tf_op jit(solution)/shard_map/ppermute | solution.py:22
  44.3 9.3 %collective-permute-done.2 = f32[7,1,18,512]{3,2,1,0:T(8,128)} collective-permute-done((f32[7,1,18,512]{3,2,1,0:T(8,128)S(1)}, f32[7,1,18,512]{3,2,1,0:T(8,128)}, u32[]{:S(2)}, u32[]{:S(2)}) %collective-permute-start.2) | collective-permute-done | bytes 258080 | tf_op jit(solution)/shard_map/ppermute | solution.py:23
  57.3 4.5 %collective-permute-start.4 = (f32[7,2,1,512]{3,2,1,0:T(1,128)S(1)}, f32[7,2,1,512]{3,2,1,0:T(1,128)S(1)}, u32[]{:S(2)}, u32[]{:S(2)}) collective-permute-start(f32[7,2,1,512]{3,2,1,0:T(1,128)S(1)} %get-tuple-element.70), channel_id=1, source_target_pairs={{0,4},{4,8},{8,12},{1,5},{5,9},{9,13},{2,6},{6,10},{10,14},{3,7},{... | collective-permute-start | bytes 86024 | tf_op jit(solution)/shard_map/ppermute | solution.py:22
  64.9 2.9 %gather_fusion.1 = f32[256,14]{1,0:T(8,128)S(1)} fusion(f32[14,8192]{0,1:T(8,128)} %copy.95, s32[1024]{0:T(1024)S(1)} %pad_clamp_fusion), kind=kCustom, calls=%fused_computation.1.clone | custom fusion | bytes 29696 | tf_op jit(solution)/shard_map/jit(_take)/gather | solution.py:164
  68.9 3.8 %all-to-all-start.2 = ((f32[8,1,896]{2,1,0:T(1,128)}), f32[8,1,896]{2,1,0:T(1,128)S(1)}, u32[]{:S(2)}, u32[]{:S(2)}) async-start(f32[8,1,896]{2,1,0:T(1,128)} %reshape.317), calls=%async_computation.2 | async-start | bytes 57344 | tf_op jit(solution)/shard_map/all_to_all | solution.py:103
  74.3 4.1 %collective-permute-start.7 = (f32[7,1,18,512]{3,2,1,0:T(8,128)}, f32[7,1,18,512]{3,2,1,0:T(8,128)}, u32[]{:S(2)}, u32[]{:S(2)}) collective-permute-start(f32[7,1,18,512]{3,2,1,0:T(8,128)} %get-tuple-element.38), channel_id=1, source_target_pairs={{0,1},{1,2},{2,3},{4,5},{5,6},{6,7},{8,9},{9,10},{10,11},{12,13},{... | collective-permute-start | bytes 774152 | tf_op jit(solution)/shard_map/ppermute | solution.py:22
  82.4 3.6 %collective-permute-done.7 = f32[7,1,18,512]{3,2,1,0:T(8,128)} collective-permute-done((f32[7,1,18,512]{3,2,1,0:T(8,128)}, f32[7,1,18,512]{3,2,1,0:T(8,128)}, u32[]{:S(2)}, u32[]{:S(2)}) %collective-permute-start.7) | collective-permute-done | bytes 258080 | tf_op jit(solution)/shard_map/ppermute | solution.py:22
  86.0 8.1 %collective-permute-done.6 = f32[7,1,18,512]{3,2,1,0:T(8,128)} collective-permute-done((f32[7,1,18,512]{3,2,1,0:T(8,128)}, f32[7,1,18,512]{3,2,1,0:T(8,128)}, u32[]{:S(2)}, u32[]{:S(2)}) %collective-permute-start.6) | collective-permute-done | bytes 258080 | tf_op jit(solution)/shard_map/ppermute | solution.py:23
  98.6 4.5 %collective-permute-start.8 = (f32[7,2,1,512]{3,2,1,0:T(1,128)S(1)}, f32[7,2,1,512]{3,2,1,0:T(1,128)S(1)}, u32[]{:S(2)}, u32[]{:S(2)}) collective-permute-start(f32[7,2,1,512]{3,2,1,0:T(1,128)S(1)} %get-tuple-element.66), channel_id=1, source_target_pairs={{0,4},{4,8},{8,12},{1,5},{5,9},{9,13},{2,6},{6,10},{10,14},{3,7},{... | collective-permute-start | bytes 86024 | tf_op jit(solution)/shard_map/ppermute | solution.py:22
  103.5 2.7 %copy.103 = f32[14,8192]{0,1:T(8,128)} copy(f32[14,8192]{1,0:T(8,128)S(1)} %bitcast.244) | data formatting | bytes 917504 | tf_op jit(solution)/shard_map/reshape | solution.py:163
  106.2 2.9 %gather_fusion.2 = f32[256,14]{1,0:T(8,128)S(1)} fusion(f32[14,8192]{0,1:T(8,128)} %copy.103, s32[1024]{0:T(1024)S(1)} %pad_clamp_fusion), kind=kCustom, calls=%fused_computation.2.clone | custom fusion | bytes 29696 | tf_op jit(solution)/shard_map/jit(_take)/gather | solution.py:164
  110.3 3.8 %all-to-all-start.3 = ((f32[8,1,896]{2,1,0:T(1,128)}), f32[8,1,896]{2,1,0:T(1,128)S(1)}, u32[]{:S(2)}, u32[]{:S(2)}) async-start(f32[8,1,896]{2,1,0:T(1,128)} %reshape.319), calls=%async_computation.3 | async-start | bytes 57344 | tf_op jit(solution)/shard_map/all_to_all | solution.py:103
  122.5 3.7 %collective-permute-done.11 = f32[7,1,18,512]{3,2,1,0:T(8,128)} collective-permute-done((f32[7,1,18,512]{3,2,1,0:T(8,128)}, f32[7,1,18,512]{3,2,1,0:T(8,128)}, u32[]{:S(2)}, u32[]{:S(2)}) %collective-permute-start.11) | collective-permute-done | bytes 258080 | tf_op jit(solution)/shard_map/ppermute | solution.py:22
  126.2 8.0 %collective-permute-done.10 = f32[7,1,18,512]{3,2,1,0:T(8,128)} collective-permute-done((f32[7,1,18,512]{3,2,1,0:T(8,128)S(1)}, f32[7,1,18,512]{3,2,1,0:T(8,128)}, u32[]{:S(2)}, u32[]{:S(2)}) %collective-permute-start.10) | collective-permute-done | bytes 258080 | tf_op jit(solution)/shard_map/ppermute | solution.py:23
  137.9 4.5 %collective-permute-start.12 = (f32[7,2,1,512]{3,2,1,0:T(1,128)S(1)}, f32[7,2,1,512]{3,2,1,0:T(1,128)S(1)}, u32[]{:S(2)}, u32[]{:S(2)}) collective-permute-start(f32[7,2,1,512]{3,2,1,0:T(1,128)S(1)} %get-tuple-element.62), channel_id=1, source_target_pairs={{0,4},{4,8},{8,12},{1,5},{5,9},{9,13},{2,6},{6,10},{10,14},{3,7},{... | collective-permute-start | bytes 86024 | tf_op jit(solution)/shard_map/ppermute | solution.py:22
  145.5 2.9 %gather_fusion.3 = f32[256,14]{1,0:T(8,128)S(1)} fusion(f32[14,8192]{0,1:T(8,128)} %copy.111, s32[1024]{0:T(1024)S(1)} %pad_clamp_fusion), kind=kCustom, calls=%fused_computation.3.clone | custom fusion | bytes 29696 | tf_op jit(solution)/shard_map/jit(_take)/gather | solution.py:164
  149.6 3.8 %all-to-all-start.4 = ((f32[8,1,896]{2,1,0:T(1,128)}), f32[8,1,896]{2,1,0:T(1,128)S(1)}, u32[]{:S(2)}, u32[]{:S(2)}) async-start(f32[8,1,896]{2,1,0:T(1,128)} %reshape.321), calls=%async_computation.4 | async-start | bytes 57344 | tf_op jit(solution)/shard_map/all_to_all | solution.py:103
  161.8 3.7 %collective-permute-done.15 = f32[7,1,18,512]{3,2,1,0:T(8,128)} collective-permute-done((f32[7,1,18,512]{3,2,1,0:T(8,128)}, f32[7,1,18,512]{3,2,1,0:T(8,128)}, u32[]{:S(2)}, u32[]{:S(2)}) %collective-permute-start.15) | collective-permute-done | bytes 258080 | tf_op jit(solution)/shard_map/ppermute | solution.py:22
  165.5 7.9 %collective-permute-done.14 = f32[7,1,18,512]{3,2,1,0:T(8,128)} collective-permute-done((f32[7,1,18,512]{3,2,1,0:T(8,128)S(1)}, f32[7,1,18,512]{3,2,1,0:T(8,128)}, u32[]{:S(2)}, u32[]{:S(2)}) %collective-permute-start.14) | collective-permute-done | bytes 258080 | tf_op jit(solution)/shard_map/ppermute | solution.py:23
  (294 shorter events, 65.9 us)
Async XLA Ops:
  0.6 21.8 %copy-start.11 = (s32[4]{0:T(128)S(1)}, s32[4]{0:T(128)}, u32[]{:S(2)}) copy-start(s32[4]{0:T(128)} %constant.34.clone) | copy-start | bytes 52
  1.8 29.4 %copy-start.9 = (f32[7]{0:T(128)S(1)}, f32[7]{0:T(128)}, u32[]{:S(2)}) copy-start(f32[7]{0:T(128)} %constant.33.clone) | copy-start | bytes 88
  1.8 29.4 %collective-permute-start.1 = (f32[7,2,1,512]{3,2,1,0:T(1,128)S(1)}, f32[7,2,1,512]{3,2,1,0:T(1,128)S(1)}, u32[]{:S(2)}, u32[]{:S(2)}) collective-permute-start(f32[7,2,1,512]{3,2,1,0:T(1,128)S(1)} %get-tuple-element.75), channel_id=1, source_target_pairs={{4,0},{8,4},{12,8},{5,1},{9,5},{13,9},{6,2},{10,6},{14,10},{7,3},{... | collective-permute-start | bytes 86024 | tf_op jit(solution)/shard_map/ppermute | solution.py:23
  3.1 28.1 %collective-permute-start = (f32[7,2,1,512]{3,2,1,0:T(1,128)S(1)}, f32[7,2,1,512]{3,2,1,0:T(1,128)S(1)}, u32[]{:S(2)}, u32[]{:S(2)}) collective-permute-start(f32[7,2,1,512]{3,2,1,0:T(1,128)S(1)} %get-tuple-element.74), channel_id=1, source_target_pairs={{0,4},{4,8},{8,12},{1,5},{5,9},{9,13},{2,6},{6,10},{10,14},{3,7},{... | collective-permute-start | bytes 86024 | tf_op jit(solution)/shard_map/ppermute | solution.py:22
  12.5 9.8 %all-to-all-start = ((f32[8,16,1]{1,2,0:T(1,128)}), f32[8,16,1]{1,2,0:T(1,128)S(1)}, u32[]{:S(2)}, u32[]{:S(2)}) async-start(f32[8,16,1]{1,2,0:T(1,128)} %bitcast.10), calls=%async_computation | async-start | bytes 8192 | tf_op jit(solution)/shard_map/all_to_all | solution.py:89
  26.7 11.3 %all-to-all-start.1 = ((f32[8,1,896]{2,1,0:T(1,128)}), f32[8,1,896]{2,1,0:T(1,128)S(1)}, u32[]{:S(2)}, u32[]{:S(2)}) async-start(f32[8,1,896]{2,1,0:T(1,128)} %reshape.315), calls=%async_computation.1 | async-start | bytes 57344 | tf_op jit(solution)/shard_map/all_to_all | solution.py:103
  32.6 11.7 %collective-permute-start.3 = (f32[7,1,18,512]{3,2,1,0:T(8,128)}, f32[7,1,18,512]{3,2,1,0:T(8,128)}, u32[]{:S(2)}, u32[]{:S(2)}) collective-permute-start(f32[7,1,18,512]{3,2,1,0:T(8,128)} %get-tuple-element.40), channel_id=1, source_target_pairs={{0,1},{1,2},{2,3},{4,5},{5,6},{6,7},{8,9},{9,10},{10,11},{12,13},{... | collective-permute-start | bytes 774152 | tf_op jit(solution)/shard_map/ppermute | solution.py:22
  36.7 16.9 %collective-permute-start.2 = (f32[7,1,18,512]{3,2,1,0:T(8,128)S(1)}, f32[7,1,18,512]{3,2,1,0:T(8,128)}, u32[]{:S(2)}, u32[]{:S(2)}) collective-permute-start(f32[7,1,18,512]{3,2,1,0:T(8,128)S(1)} %get-tuple-element.41), channel_id=1, source_target_pairs={{1,0},{2,1},{3,2},{5,4},{6,5},{7,6},{9,8},{10,9},{11,10},{13,12},{... | collective-permute-start | bytes 774152 | tf_op jit(solution)/shard_map/ppermute | solution.py:23
  56.0 16.8 %collective-permute-start.5 = (f32[7,2,1,512]{3,2,1,0:T(1,128)S(1)}, f32[7,2,1,512]{3,2,1,0:T(1,128)S(1)}, u32[]{:S(2)}, u32[]{:S(2)}) collective-permute-start(f32[7,2,1,512]{3,2,1,0:T(1,128)S(1)} %get-tuple-element.71), channel_id=1, source_target_pairs={{4,0},{8,4},{12,8},{5,1},{9,5},{13,9},{6,2},{10,6},{14,10},{7,3},{... | collective-permute-start | bytes 86024 | tf_op jit(solution)/shard_map/ppermute | solution.py:23
  57.3 15.5 %collective-permute-start.4 = (f32[7,2,1,512]{3,2,1,0:T(1,128)S(1)}, f32[7,2,1,512]{3,2,1,0:T(1,128)S(1)}, u32[]{:S(2)}, u32[]{:S(2)}) collective-permute-start(f32[7,2,1,512]{3,2,1,0:T(1,128)S(1)} %get-tuple-element.70), channel_id=1, source_target_pairs={{0,4},{4,8},{8,12},{1,5},{5,9},{9,13},{2,6},{6,10},{10,14},{3,7},{... | collective-permute-start | bytes 86024 | tf_op jit(solution)/shard_map/ppermute | solution.py:22
  68.9 10.8 %all-to-all-start.2 = ((f32[8,1,896]{2,1,0:T(1,128)}), f32[8,1,896]{2,1,0:T(1,128)S(1)}, u32[]{:S(2)}, u32[]{:S(2)}) async-start(f32[8,1,896]{2,1,0:T(1,128)} %reshape.317), calls=%async_computation.2 | async-start | bytes 57344 | tf_op jit(solution)/shard_map/all_to_all | solution.py:103
  74.3 21.1 %copy-start.3 = (f32[7,2,18,512]{3,2,1,0:T(8,128)}, f32[7,2,18,512]{3,2,1,0:T(8,128)S(1)}, u32[]{:S(2)}) copy-start(f32[7,2,18,512]{3,2,1,0:T(8,128)S(1)} %constant_dynamic-update-slice_fusion.49) | copy-start | bytes 1548292
  74.3 11.7 %collective-permute-start.7 = (f32[7,1,18,512]{3,2,1,0:T(8,128)}, f32[7,1,18,512]{3,2,1,0:T(8,128)}, u32[]{:S(2)}, u32[]{:S(2)}) collective-permute-start(f32[7,1,18,512]{3,2,1,0:T(8,128)} %get-tuple-element.38), channel_id=1, source_target_pairs={{0,1},{1,2},{2,3},{4,5},{5,6},{6,7},{8,9},{9,10},{10,11},{12,13},{... | collective-permute-start | bytes 774152 | tf_op jit(solution)/shard_map/ppermute | solution.py:22
  78.5 15.7 %collective-permute-start.6 = (f32[7,1,18,512]{3,2,1,0:T(8,128)}, f32[7,1,18,512]{3,2,1,0:T(8,128)}, u32[]{:S(2)}, u32[]{:S(2)}) collective-permute-start(f32[7,1,18,512]{3,2,1,0:T(8,128)} %get-tuple-element.39), channel_id=1, source_target_pairs={{1,0},{2,1},{3,2},{5,4},{6,5},{7,6},{9,8},{10,9},{11,10},{13,12},{... | collective-permute-start | bytes 774152 | tf_op jit(solution)/shard_map/ppermute | solution.py:23
  97.3 16.8 %collective-permute-start.9 = (f32[7,2,1,512]{3,2,1,0:T(1,128)S(1)}, f32[7,2,1,512]{3,2,1,0:T(1,128)S(1)}, u32[]{:S(2)}, u32[]{:S(2)}) collective-permute-start(f32[7,2,1,512]{3,2,1,0:T(1,128)S(1)} %get-tuple-element.67), channel_id=1, source_target_pairs={{4,0},{8,4},{12,8},{5,1},{9,5},{13,9},{6,2},{10,6},{14,10},{7,3},{... | collective-permute-start | bytes 86024 | tf_op jit(solution)/shard_map/ppermute | solution.py:23
  98.6 15.5 %collective-permute-start.8 = (f32[7,2,1,512]{3,2,1,0:T(1,128)S(1)}, f32[7,2,1,512]{3,2,1,0:T(1,128)S(1)}, u32[]{:S(2)}, u32[]{:S(2)}) collective-permute-start(f32[7,2,1,512]{3,2,1,0:T(1,128)S(1)} %get-tuple-element.66), channel_id=1, source_target_pairs={{0,4},{4,8},{8,12},{1,5},{5,9},{9,13},{2,6},{6,10},{10,14},{3,7},{... | collective-permute-start | bytes 86024 | tf_op jit(solution)/shard_map/ppermute | solution.py:22
  110.3 9.6 %all-to-all-start.3 = ((f32[8,1,896]{2,1,0:T(1,128)}), f32[8,1,896]{2,1,0:T(1,128)S(1)}, u32[]{:S(2)}, u32[]{:S(2)}) async-start(f32[8,1,896]{2,1,0:T(1,128)} %reshape.319), calls=%async_computation.3 | async-start | bytes 57344 | tf_op jit(solution)/shard_map/all_to_all | solution.py:103
  116.4 9.8 %collective-permute-start.11 = (f32[7,1,18,512]{3,2,1,0:T(8,128)}, f32[7,1,18,512]{3,2,1,0:T(8,128)}, u32[]{:S(2)}, u32[]{:S(2)}) collective-permute-start(f32[7,1,18,512]{3,2,1,0:T(8,128)} %get-tuple-element.36), channel_id=1, source_target_pairs={{0,1},{1,2},{2,3},{4,5},{5,6},{6,7},{8,9},{9,10},{10,11},{12,13},{... | collective-permute-start | bytes 774152 | tf_op jit(solution)/shard_map/ppermute | solution.py:22
  118.6 15.6 %collective-permute-start.10 = (f32[7,1,18,512]{3,2,1,0:T(8,128)S(1)}, f32[7,1,18,512]{3,2,1,0:T(8,128)}, u32[]{:S(2)}, u32[]{:S(2)}) collective-permute-start(f32[7,1,18,512]{3,2,1,0:T(8,128)S(1)} %get-tuple-element.37), channel_id=1, source_target_pairs={{1,0},{2,1},{3,2},{5,4},{6,5},{7,6},{9,8},{10,9},{11,10},{13,12},{... | collective-permute-start | bytes 774152 | tf_op jit(solution)/shard_map/ppermute | solution.py:23
  136.6 16.8 %collective-permute-start.13 = (f32[7,2,1,512]{3,2,1,0:T(1,128)S(1)}, f32[7,2,1,512]{3,2,1,0:T(1,128)S(1)}, u32[]{:S(2)}, u32[]{:S(2)}) collective-permute-start(f32[7,2,1,512]{3,2,1,0:T(1,128)S(1)} %get-tuple-element.63), channel_id=1, source_target_pairs={{4,0},{8,4},{12,8},{5,1},{9,5},{13,9},{6,2},{10,6},{14,10},{7,3},{... | collective-permute-start | bytes 86024 | tf_op jit(solution)/shard_map/ppermute | solution.py:23
  137.9 15.5 %collective-permute-start.12 = (f32[7,2,1,512]{3,2,1,0:T(1,128)S(1)}, f32[7,2,1,512]{3,2,1,0:T(1,128)S(1)}, u32[]{:S(2)}, u32[]{:S(2)}) collective-permute-start(f32[7,2,1,512]{3,2,1,0:T(1,128)S(1)} %get-tuple-element.62), channel_id=1, source_target_pairs={{0,4},{4,8},{8,12},{1,5},{5,9},{9,13},{2,6},{6,10},{10,14},{3,7},{... | collective-permute-start | bytes 86024 | tf_op jit(solution)/shard_map/ppermute | solution.py:22
  149.6 9.6 %all-to-all-start.4 = ((f32[8,1,896]{2,1,0:T(1,128)}), f32[8,1,896]{2,1,0:T(1,128)S(1)}, u32[]{:S(2)}, u32[]{:S(2)}) async-start(f32[8,1,896]{2,1,0:T(1,128)} %reshape.321), calls=%async_computation.4 | async-start | bytes 57344 | tf_op jit(solution)/shard_map/all_to_all | solution.py:103
  155.7 9.8 %collective-permute-start.15 = (f32[7,1,18,512]{3,2,1,0:T(8,128)}, f32[7,1,18,512]{3,2,1,0:T(8,128)}, u32[]{:S(2)}, u32[]{:S(2)}) collective-permute-start(f32[7,1,18,512]{3,2,1,0:T(8,128)} %get-tuple-element.34), channel_id=1, source_target_pairs={{0,1},{1,2},{2,3},{4,5},{5,6},{6,7},{8,9},{9,10},{10,11},{12,13},{... | collective-permute-start | bytes 774152 | tf_op jit(solution)/shard_map/ppermute | solution.py:22
  157.8 15.6 %collective-permute-start.14 = (f32[7,1,18,512]{3,2,1,0:T(8,128)S(1)}, f32[7,1,18,512]{3,2,1,0:T(8,128)}, u32[]{:S(2)}, u32[]{:S(2)}) collective-permute-start(f32[7,1,18,512]{3,2,1,0:T(8,128)S(1)} %get-tuple-element.35), channel_id=1, source_target_pairs={{1,0},{2,1},{3,2},{5,4},{6,5},{7,6},{9,8},{10,9},{11,10},{13,12},{... | collective-permute-start | bytes 774152 | tf_op jit(solution)/shard_map/ppermute | solution.py:23
  (9 other events, 86.8 us)
where the time goes:
time: 179 us; the launch traced here: 177 us
  starting transfers between devices  62.3 us (35%)
  waiting for transfers between devices  48.2 us (27%)
  local copies, waits for them, and re-layouts  40.8 us (23%)
  other arithmetic  21 us (12%)
  matrix products  3.16 us (2%)
  between operations  2.03 us (1%)
    ppermute x8, waiting for transfers between devices, padded(): after = lax.ppermute(first, axis, down)  33.3 us
    ppermute x8, starting transfers between devices, padded(): before = lax.ppermute(last, axis, up)  31.8 us
    all_to_all x4, starting transfers between devices, route_reply(): lax.all_to_all(doubled, ('panel', 'ang'), split_axis=1, concat_axis=1, ti...  15.9 us
    ppermute x8, waiting for transfers between devices, padded(): before = lax.ppermute(last, axis, up)  14.1 us
    gather x4, local copies, waits for them, and re-layouts, overset(): jnp.take(table, gather_index, axis=1).reshape(stacked_rows, slot_count, 4)  11.6 us
    reshape x4, local copies, waits for them, and re-layouts, overset(): table = current.reshape(stacked_rows, rows_p * rows_t)  10.7 us
    ppermute x8, starting transfers between devices, padded(): after = lax.ppermute(first, axis, down)  10.3 us
    unnamed x64, local copies, waits for them, and re-layouts  8.22 us
  transfers between devices with their start and end apart: 21, of which 10 were waited for; matrix products, arithmetic and copies ran while one was open for 28% of the time, Pallas kernels for 0%

commit v1 on v0

v1 whole, which is shorter than its diff:
```python
import functools
import math

import jax
import jax.numpy as jnp
from jax import lax
from jax.experimental import pallas as pl
from jax.experimental.pallas import tpu as pltpu
from jax.sharding import PartitionSpec as P

time_step = 0.15
mixing = (0.0, 0.1, 0.1, 0.1, 0.1, 0.1, 0.1)
wall = (1.0, -1.0, -1.0, -1.0, 1.0, 1.0, 1.0)
r_inner = 0.35
FIELDS = 7
LANES = 128
LEVELS = 8
ahead = (0.5 * time_step, 0.5 * time_step, time_step)
share = (time_step / 6.0, time_step / 3.0, time_step / 3.0, time_step / 6.0)


def point_values(u):
    rate = 1.0 / u[0]
    speed = [u[1 + c] * rate for c in range(3)]
    pressure = u[0] + 0.5 * (u[4] * u[4] + u[5] * u[5] + u[6] * u[6])
    return speed, pressure


def flux_of(u, speed, pressure, d, stress, twist):
    out = [u[1 + d]]
    for c in range(3):
        key = (min(c, d), max(c, d))
        if key not in stress:
            term = u[1 + c] * speed[d] - u[4 + c] * u[4 + d]
            stress[key] = term + pressure if c == d else term
        out.append(stress[key])
    for c in range(3):
        if c == d:
            out.append(None)
            continue
        key = (min(c, d), max(c, d))
        if key not in twist:
            low, high = key
            twist[key] = speed[high] * u[4 + low] - u[4 + high] * speed[low]
        out.append(twist[key] if c == key[0] else -twist[key])
    return out


def low_high(u, flux, half, mix):
    low, high = [], []
    for f in range(FIELDS):
        carried = None if flux[f] is None else half * flux[f]
        spread = None if mixing[f] == 0.0 else mix * u[f]
        if carried is None:
            low.append(spread)
            high.append(spread)
        elif spread is None:
            low.append(carried)
            high.append(-carried)
        else:
            low.append(spread + carried)
            high.append(spread - carried)
    return low, high


def kernel(
    sizes,
    den, mom, mag, pdev, pphi, ptheta, pweight, pturn,
    oden, omom, omag,
    land, staged, state, total, slope, x_low, x_high, geo,
    phi_in, theta_out, theta_in, over_out, over_in,
    meta_out, meta_in, coef, picker,
    own_sem, load_send, load_recv, give_send, give_recv,
    meta_send, meta_recv, phi_send, phi_recv, theta_send, theta_recv,
    over_send, over_recv,
):
    n_ang, n_rad, rows, cells, border = sizes
    side_rows = border // 2
    per_tile = LANES // border
    tiles = n_ang // per_tile
    sources = n_ang * n_rad
    mine = lax.axis_index("panel")
    a = lax.axis_index("ang")
    t = lax.axis_index("rad")
    other = 1 - mine

    def at(panel, ang, rad):
        return {"panel": panel, "ang": ang, "rad": rad}

    barrier = pltpu.get_barrier_semaphore()

    def greet(i, carry):
        pl.semaphore_signal(
            barrier, inc=1,
            device_id=at(other, i // n_rad, lax.rem(i, n_rad)),
            device_id_type=pl.DeviceIdType.MESH,
        )
        return carry

    lax.fori_loop(0, sources, greet, 0)
    for step in range(1, n_rad):
        pl.semaphore_signal(
            barrier, inc=1, device_id=at(mine, a, lax.rem(t + step, n_rad)),
            device_id_type=pl.DeviceIdType.MESH,
        )

    @pl.when(a > 0)
    def _():
        pl.semaphore_signal(
            barrier, inc=1, device_id=at(mine, a - 1, t), device_id_type=pl.DeviceIdType.MESH
        )

    @pl.when(a < n_ang - 1)
    def _():
        pl.semaphore_signal(
            barrier, inc=1, device_id=at(mine, a + 1, t), device_id_type=pl.DeviceIdType.MESH
        )

    own_rows = pl.ds(pl.multiple_of(t * rows, rows), rows)
    own_lanes = pl.ds(pl.multiple_of(t * LANES, LANES), LANES)
    own = [
        pltpu.make_async_copy(den.at[:, own_lanes], land.at[0, own_rows, :], own_sem.at[0]),
        pltpu.make_async_copy(mom.at[:, :, own_lanes], land.at[pl.ds(1, 3), own_rows, :], own_sem.at[1]),
        pltpu.make_async_copy(mag.at[:, :, own_lanes], land.at[pl.ds(4, 3), own_rows, :], own_sem.at[2]),
    ]
    for copy in own:
        copy.start()

    sub8 = lax.broadcasted_iota(jnp.int32, (LEVELS, LANES), 0)
    lane8 = lax.broadcasted_iota(jnp.int32, (LEVELS, LANES), 1)
    sub_b = lax.broadcasted_iota(jnp.int32, (border, LANES), 0)
    lane_b = lax.broadcasted_iota(jnp.int32, (border, LANES), 1)
    square = (
        lax.broadcasted_iota(jnp.int32, (border, border), 0)
        == lax.broadcasted_iota(jnp.int32, (border, border), 1)
    )

    def column(row):
        wide = jnp.broadcast_to(row, (border, border))
        return jnp.sum(jnp.where(square, wide, 0.0), axis=1, keepdims=True)

    place = lane_b == sub_b + border * lax.rem(a, per_tile)
    columns = [
        pdev[...].astype(jnp.float32),
        column(pphi[...].astype(jnp.float32)),
        column(ptheta[...].astype(jnp.float32)),
    ] + [pweight[:, i:i + 1] for i in range(4)]
    meta_out[...] = jnp.zeros_like(meta_out)
    for i, col in enumerate(columns):
        meta_out[i:i + 1, :] = jnp.sum(
            jnp.where(place, jnp.broadcast_to(col, (border, LANES)), 0.0), axis=0, keepdims=True
        )

    at_low = t == 0
    at_high = t == n_rad - 1
    base_row = jnp.where(at_high, side_rows, 0)
    turn_at = sub_b == base_row + lax.rem(lane_b, side_rows)
    angle = jnp.sum(
        jnp.where(turn_at, jnp.broadcast_to(column(pturn[...]), (border, LANES)), 0.0),
        axis=0, keepdims=True,
    )
    angle = jnp.broadcast_to(angle, (LEVELS, LANES))
    cosine, sine = jnp.cos(angle), jnp.sin(angle)

    radius = r_inner + (sub8.astype(jnp.float32) + 0.5) * ((1.0 - r_inner) / LEVELS)
    theta = math.pi / 4 + ((lane8 + t * LANES).astype(jnp.float32) + 0.5) * (
        math.pi / 2 / (LANES * n_rad)
    )
    inv_radius = 1.0 / radius
    inv_both = inv_radius / jnp.sin(theta)
    half_t = 0.5 * inv_radius
    mix_t = 0.1 * inv_radius * inv_radius
    half_p = 0.5 * inv_both
    mix_p = 0.1 * inv_both * inv_both
    centre = -2.0 * (0.1 + mix_t + mix_p)
    for i, value in enumerate((half_t, mix_t, half_p, mix_p, centre)):
        geo[i] = value

    pl.semaphore_wait(
        barrier,
        sources + n_rad - 1 + jnp.where(a > 0, 1, 0) + jnp.where(a < n_ang - 1, 1, 0),
    )

    loads = []
    for step in range(1, n_rad):
        to = lax.rem(t + step, n_rad)
        lanes = pl.ds(pl.multiple_of(to * LANES, LANES), LANES)
        for i, (src, dst) in enumerate((
            (den.at[:, lanes], land.at[0, own_rows, :]),
            (mom.at[:, :, lanes], land.at[pl.ds(1, 3), own_rows, :]),
            (mag.at[:, :, lanes], land.at[pl.ds(4, 3), own_rows, :]),
        )):
            loads.append(pltpu.make_async_remote_copy(
                src_ref=src, dst_ref=dst,
                send_sem=load_send.at[i, step], recv_sem=load_recv.at[i, step],
                device_id=at(mine, a, to), device_id_type=pl.DeviceIdType.MESH,
            ))
    for copy in loads:
        copy.start()

    def meta_copy(to):
        return pltpu.make_async_remote_copy(
            src_ref=meta_out, dst_ref=meta_in.at[a],
            send_sem=meta_send, recv_sem=meta_recv,
            device_id=at(other, to, t), device_id_type=pl.DeviceIdType.MESH,
        )

    def send_meta(to, carry):
        meta_copy(to).start()
        return carry

    lax.fori_loop(0, n_ang, send_meta, 0)
    pltpu.make_async_copy(meta_in, meta_in, meta_recv).wait()

    sub_l = lax.broadcasted_iota(jnp.int32, (LANES, LANES), 0)
    sub_c = lax.broadcasted_iota(jnp.int32, (cells, LANES), 0)

    def prepare(g, carry):
        table = jnp.sum(meta_in[pl.ds(g * per_tile, per_tile)], axis=0)
        device = table[0:1].astype(jnp.int32)
        at_phi = table[1:2].astype(jnp.int32)
        at_theta = table[2:3].astype(jnp.int32) - t * LANES
        hit = jnp.broadcast_to(device == a, (cells, LANES))
        near = hit & (sub_c == at_phi)
        far = hit & (sub_c == at_phi + 1)
        zero = jnp.zeros((cells, LANES), jnp.float32)
        w = [jnp.broadcast_to(table[3 + i:4 + i], (cells, LANES)) for i in range(4)]
        coef[g, 0] = jnp.where(near, w[0], jnp.where(far, w[2], zero))
        coef[g, 1] = jnp.where(near, w[1], jnp.where(far, w[3], zero))
        first = jnp.where(sub_l == at_theta, 1.0, 0.0).astype(jnp.bfloat16)
        second = jnp.where(sub_l == at_theta + 1, 1.0, 0.0).astype(jnp.bfloat16)
        for part in range(2):
            picker[g, pl.ds(part * LANES, LANES), pl.ds(0, LANES)] = first
            picker[g, pl.ds(part * LANES, LANES), pl.ds(LANES, LANES)] = second
        return carry

    if tiles == 1:
        prepare(0, 0)
    else:
        lax.fori_loop(0, tiles, prepare, 0)

    for copy in own:
        copy.wait()
    for copy in loads:
        copy.wait_recv()

    block_of = lane8 // side_rows
    first_lane = lane8 == 0
    last_lane = lane8 == LANES - 1
    first_level = sub8 == 0
    last_level = sub8 == LEVELS - 1

    def pack(k, f, value, packs):
        low, high = packs
        spot = f * cells + k
        hit = lane8 == spot
        low = jnp.where(hit, pltpu.roll(value, spot, 1), low)
        high = jnp.where(hit, pltpu.roll(value, spot + 1, 1), high)
        return low, high

    def phi_copies(s):
        down = pltpu.make_async_remote_copy(
            src_ref=state.at[s, 0], dst_ref=phi_in.at[s, 1],
            send_sem=phi_send.at[s, 0], recv_sem=phi_recv.at[s, 1],
            device_id=at(mine, a, t) | {"ang": jnp.maximum(a - 1, 0)},
            device_id_type=pl.DeviceIdType.MESH,
        )
        up = pltpu.make_async_remote_copy(
            src_ref=state.at[s, cells - 1], dst_ref=phi_in.at[s, 0],
            send_sem=phi_send.at[s, 1], recv_sem=phi_recv.at[s, 0],
            device_id=at(mine, a, t) | {"ang": jnp.minimum(a + 1, n_ang - 1)},
            device_id_type=pl.DeviceIdType.MESH,
        )
        return down, up

    def theta_copies(s):
        down = pltpu.make_async_remote_copy(
            src_ref=theta_out.at[s, 0], dst_ref=theta_in.at[s, 1],
            send_sem=theta_send.at[s, 0], recv_sem=theta_recv.at[s, 1],
            device_id=at(mine, a, jnp.maximum(t - 1, 0)),
            device_id_type=pl.DeviceIdType.MESH,
        )
        up = pltpu.make_async_remote_copy(
            src_ref=theta_out.at[s, 1], dst_ref=theta_in.at[s, 0],
            send_sem=theta_send.at[s, 1], recv_sem=theta_recv.at[s, 0],
            device_id=at(mine, a, jnp.minimum(t + 1, n_rad - 1)),
            device_id_type=pl.DeviceIdType.MESH,
        )
        return down, up

    def over_copy(s, q):
        return pltpu.make_async_remote_copy(
            src_ref=over_out.at[s, q], dst_ref=over_in.at[s, a * n_rad + t],
            send_sem=over_send.at[s], recv_sem=over_recv.at[s],
            device_id=at(other, q // 2, lax.rem(q, 2) * (n_rad - 1)),
            device_id_type=pl.DeviceIdType.MESH,
        )

    def send_all(s, packs):
        theta_out[s, 0], theta_out[s, 1] = packs
        theta_down, theta_up = theta_copies(s)
        phi_down, phi_up = phi_copies(s)
        for can, copy in (
            (t > 0, theta_down), (t < n_rad - 1, theta_up),
            (a > 0, phi_down), (a < n_ang - 1, phi_up),
        ):
            pl.when(can)(copy.start)

        def overset(g, carry):
            turned = []
            for f in range(FIELDS):
                value = state[s, :, f].reshape(cells * LEVELS, LANES)
                head = value.astype(jnp.bfloat16)
                rest = (value - head.astype(jnp.float32)).astype(jnp.bfloat16)
                got = jnp.dot(
                    jnp.concatenate([head, rest], axis=1), picker[g],
                    preferred_element_type=jnp.float32,
                )
                ghost = None
                for k in range(cells):
                    piece = got[k * LEVELS:(k + 1) * LEVELS]
                    term = (
                        piece[:, :LANES] * coef[g, 0, k:k + 1, :]
                        + piece[:, LANES:] * coef[g, 1, k:k + 1, :]
                    )
                    ghost = term if ghost is None else ghost + term
                turned.append(pltpu.roll(ghost, f * side_rows, 1) if f else ghost)
            groups = LANES // side_rows
            for j in range(groups):
                message = turned[0]
                for f in range(FIELDS):
                    message = jnp.where(block_of == (f + j) % groups, turned[f], message)
                if j:
                    message = pltpu.roll(message, LANES - j * side_rows, 1)
                over_out[s, g * groups + j] = message
            for j in range(groups):
                over_copy(s, g * groups + j).start()
            return carry

        if tiles == 1:
            overset(0, 0)
        else:
            lax.fori_loop(0, tiles, overset, 0)

    def inner(s):
        half_t, mix_t, half_p, mix_p, centre = [geo[i] for i in range(5)]

        def row(k, carry):
            u = [state[s, k, f] for f in range(FIELDS)]
            speed, pressure = point_values(u)
            stress, twist = {}, {}
            low_r, high_r = low_high(u, flux_of(u, speed, pressure, 0, stress, twist), 0.5, 0.1)
            low_t, high_t = low_high(u, flux_of(u, speed, pressure, 1, stress, twist), half_t, mix_t)
            low_p, high_p = low_high(u, flux_of(u, speed, pressure, 2, stress, twist), half_p, mix_p)
            for f in range(FIELDS):
                below = pltpu.roll(low_r[f], 1, 0)
                above = pltpu.roll(high_r[f], LEVELS - 1, 0)
                below = jnp.where(first_level, wall[f] * high_r[f], below)
                above = jnp.where(last_level, wall[f] * low_r[f], above)
                left = jnp.where(first_lane, 0.0, pltpu.roll(low_t[f], 1, 1))
                right = jnp.where(last_lane, 0.0, pltpu.roll(high_t[f], LANES - 1, 1))
                value = (below + above) + (left + right)
                if mixing[f] != 0.0:
                    value = value + centre * u[f]
                slope[k, f] = value
                x_low[k + 1, f] = low_p[f]
                x_high[k + 1, f] = high_p[f]
            return carry

        lax.fori_loop(0, cells, row, 0, unroll=2)

    def halos(s):
        half_t, mix_t, half_p, mix_p, centre = [geo[i] for i in range(5)]
        phi_down, phi_up = phi_copies(s)
        theta_down, theta_up = theta_copies(s)

        def beside(side):
            u = [phi_in[s, side, f] for f in range(FIELDS)]
            speed, pressure = point_values(u)
            low, high = low_high(u, flux_of(u, speed, pressure, 2, {}, {}), half_p, mix_p)
            for f in range(FIELDS):
                if side == 0:
                    x_low[0, f] = low[f]
                else:
                    x_high[cells + 1, f] = high[f]

        @pl.when(a > 0)
        def _():
            phi_up.wait_recv()
            beside(0)

        @pl.when(a == 0)
        def _():
            for f in range(FIELDS):
                x_low[0, f] = wall[f] * x_high[1, f]

        @pl.when(a < n_ang - 1)
        def _():
            phi_down.wait_recv()
            beside(1)

        @pl.when(a == n_ang - 1)
        def _():
            for f in range(FIELDS):
                x_high[cells + 1, f] = wall[f] * x_low[cells, f]

        @pl.when(t > 0)
        def _():
            theta_up.wait_recv()

        @pl.when(t < n_rad - 1)
        def _():
            theta_down.wait_recv()

        @pl.when(at_low | at_high)
        def _():
            pltpu.make_async_copy(over_in.at[s], over_in.at[s], over_recv.at[s]).wait()
            ghost = jnp.sum(over_in[s], axis=0)
            nexts = pltpu.roll(ghost, LANES - side_rows, 1)
            lasts = pltpu.roll(ghost, side_rows, 1)
            is_theta = (block_of == 2) | (block_of == 5)
            is_phi = (block_of == 3) | (block_of == 6)
            ghost = jnp.where(
                is_theta, cosine * ghost + sine * nexts,
                jnp.where(is_phi, cosine * ghost - sine * lasts, ghost),
            )

            @pl.when(at_low)
            def _():
                theta_in[s, 0] = ghost

            @pl.when(at_high)
            def _():
                theta_in[s, 1] = ghost

        lower, upper = theta_in[s, 0], theta_in[s, 1]
        half_lane = LANES // 2
        is_low = lane8 < half_lane
        u = []
        for f in range(FIELDS):
            here = pltpu.roll(lower, LANES - f * cells, 1) if f else lower
            there = pltpu.roll(upper, (half_lane - f * cells) % LANES, 1)
            u.append(jnp.where(is_low, here, there))
        speed, pressure = point_values(u)
        signed = jnp.where(is_low, half_t, -half_t)
        edge, _ = low_high(u, flux_of(u, speed, pressure, 1, {}, {}), signed, mix_t)
        return edge

    def tend(k, f, edge):
        low = pltpu.roll(edge[f], lax.rem(LANES - k, LANES), 1)
        high = pltpu.roll(edge[f], LANES // 2 - 1 - k, 1)
        ends = jnp.where(first_lane, low, jnp.where(last_lane, high, 0.0))
        return (slope[k, f] + ends) + (x_low[k, f] + x_high[k + 2, f])

    zero8 = jnp.zeros((LEVELS, LANES), jnp.float32)

    def enter(k, packs):
        for f in range(FIELDS):
            value = land[f, pl.ds(k, LEVELS, stride=cells), :]
            state[0, k, f] = value
            packs = pack(k, f, value, packs)
        return packs

    packs = lax.fori_loop(0, cells, enter, (zero8, zero8), unroll=True)

    for s in range(4):
        send_all(s, packs)
        inner(s)
        edge = halos(s)
        if s < 3:
            def advance(k, packs):
                for f in range(FIELDS):
                    base = state[0, k, f]
                    k_now = tend(k, f, edge)
                    value = base + ahead[s] * k_now
                    state[s + 1, k, f] = value
                    packs = pack(k, f, value, packs)
                    total[k, f] = (base if s == 0 else total[k, f]) + share[s] * k_now
                return packs

            packs = lax.fori_loop(0, cells, advance, (zero8, zero8), unroll=True)
        else:
            def finish(k, carry):
                for f in range(FIELDS):
                    value = total[k, f] + share[s] * tend(k, f, edge)
                    staged[f, pl.ds(k, LEVELS, stride=cells), :] = value
                return carry

            lax.fori_loop(0, cells, finish, 0, unroll=True)

    gives = []
    for step in range(1, n_rad):
        to = lax.rem(t + step, n_rad)
        there = pl.ds(pl.multiple_of(to * rows, rows), rows)
        for i, (src, dst) in enumerate((
            (staged.at[0, there, :], oden.at[:, own_lanes]),
            (staged.at[pl.ds(1, 3), there, :], omom.at[:, :, own_lanes]),
            (staged.at[pl.ds(4, 3), there, :], omag.at[:, :, own_lanes]),
        )):
            gives.append(pltpu.make_async_remote_copy(
                src_ref=src, dst_ref=dst,
                send_sem=give_send.at[i, step], recv_sem=give_recv.at[i, step],
                device_id=at(mine, a, to), device_id_type=pl.DeviceIdType.MESH,
            ))
    for copy in gives:
        copy.start()
    keeps = [
        pltpu.make_async_copy(staged.at[0, own_rows, :], oden.at[:, own_lanes], own_sem.at[0]),
        pltpu.make_async_copy(staged.at[pl.ds(1, 3), own_rows, :], omom.at[:, :, own_lanes], own_sem.at[1]),
        pltpu.make_async_copy(staged.at[pl.ds(4, 3), own_rows, :], omag.at[:, :, own_lanes], own_sem.at[2]),
    ]
    for copy in keeps:
        copy.start()

    for copy in loads:
        copy.wait_send()
    pltpu.make_async_copy(meta_in, meta_in, meta_send).wait()
    for s in range(4):
        phi_down, phi_up = phi_copies(s)
        theta_down, theta_up = theta_copies(s)
        for can, copy in (
            (t > 0, theta_down), (t < n_rad - 1, theta_up),
            (a > 0, phi_down), (a < n_ang - 1, phi_up),
        ):
            pl.when(can)(copy.wait_send)
        pltpu.make_async_copy(over_out.at[s], over_out.at[s], over_send.at[s]).wait()
    for copy in keeps:
        copy.wait()
    for copy in gives:
        copy.wait()


def body(density, momentum, magnetic, partner_device, partner_phi, partner_theta, partner_weight,
         border_turn):
    _, rows_r, cells, n_theta = density.shape
    border = partner_phi.shape[1]
    n_ang, n_rad = lax.axis_size("ang"), lax.axis_size("rad")
    rows = rows_r * cells
    assert rows_r * n_rad == LEVELS and n_theta == LANES * n_rad and n_rad > 1
    assert LANES % border == 0 and n_ang % (LANES // border) == 0 and border == 2 * cells
    f32 = jnp.float32
    tiles = n_ang * border // LANES
    sources = n_ang * n_rad
    vmem = pltpu.VMEM
    dma = pltpu.SemaphoreType.DMA
    spaces = [pl.BlockSpec(memory_space=pl.ANY)] * 3 + [pl.BlockSpec(memory_space=vmem)] * 5
    outs = pl.pallas_call(
        functools.partial(kernel, (n_ang, n_rad, rows, cells, border)),
        out_shape=(
            jax.ShapeDtypeStruct((rows, n_theta), f32),
            jax.ShapeDtypeStruct((3, rows, n_theta), f32),
            jax.ShapeDtypeStruct((3, rows, n_theta), f32),
        ),
        in_specs=spaces,
        out_specs=[pl.BlockSpec(memory_space=pl.ANY)] * 3,
        scratch_shapes=[
            vmem((FIELDS, LEVELS * cells, LANES), f32),
            vmem((FIELDS, LEVELS * cells, LANES), f32),
            vmem((4, cells, FIELDS, LEVELS, LANES), f32),
            vmem((cells, FIELDS, LEVELS, LANES), f32),
            vmem((cells, FIELDS, LEVELS, LANES), f32),
            vmem((cells + 2, FIELDS, LEVELS, LANES), f32),
            vmem((cells + 2, FIELDS, LEVELS, LANES), f32),
            vmem((5, LEVELS, LANES), f32),
            vmem((4, 2, FIELDS, LEVELS, LANES), f32),
            vmem((4, 2, LEVELS, LANES), f32),
            vmem((4, 2, LEVELS, LANES), f32),
            vmem((4, 2 * n_ang, LEVELS, LANES), f32),
            vmem((4, sources, LEVELS, LANES), f32),
            vmem((LEVELS, LANES), f32),
            vmem((n_ang, LEVELS, LANES), f32),
            vmem((tiles, 2, cells, LANES), f32),
            vmem((tiles, 2 * LANES, 2 * LANES), jnp.bfloat16),
            dma((3,)), dma((3, n_rad)), dma((3, n_rad)), dma((3, n_rad)), dma((3, n_rad)),
            dma, dma, dma((4, 2)), dma((4, 2)), dma((4, 2)), dma((4, 2)), dma((4,)), dma((4,)),
        ],
        compiler_params=pltpu.CompilerParams(
            collective_id=0, has_side_effects=True, vmem_limit_bytes=32 * 1024 * 1024
        ),
    )(
        density.reshape(rows, n_theta),
        momentum.reshape(3, rows, n_theta),
        magnetic.reshape(3, rows, n_theta),
        partner_device.reshape(border, 1),
        partner_phi, partner_theta,
        partner_weight.reshape(border, 4),
        border_turn,
    )
    return (
        outs[0].reshape(density.shape),
        outs[1].reshape(momentum.shape),
        outs[2].reshape(magnetic.shape),
    )


def solution(mesh):
    in_specs = (
        P("panel", "rad", "ang", None),
        P("panel", None, "rad", "ang", None),
        P("panel", None, "rad", "ang", None),
        P("panel", "ang", None),
        P("panel", "ang"),
        P("panel", "ang"),
        P("panel", "ang", None),
        P("panel", "ang"),
    )
    out_specs = (
        P("panel", "rad", "ang", None),
        P("panel", None, "rad", "ang", None),
        P("panel", None, "rad", "ang", None),
    )
    return jax.shard_map(body, mesh=mesh, in_specs=in_specs, out_specs=out_specs, check_vma=False)
```

time: 179 us -> 49.5 us (0.28)
  starting transfers between devices: 62.3 us -> 0 us
  waiting for transfers between devices: 48.2 us -> 0 us
  Pallas kernels: 0 us -> 41.9 us
  local copies, waits for them, and re-layouts: 40.8 us -> 6.69 us
  other arithmetic: 21 us -> 0 us
  matrix products: 3.16 us -> 0 us
    ppermute x16 -> x0, waiting for transfers between devices: 47.4 us -> none  [the longest x8 33.3 us: padded(): after = lax.ppermute(first, axis, down)]
    ppermute x16 -> x0, starting transfers between devices: 42.1 us -> none  [the longest x8 31.8 us: padded(): before = lax.ppermute(last, axis, up)]
    pallas_call x0 -> x1, Pallas kernels: none -> 41.9 us  [body(): pl.pallas_call(functools.partial(kernel, (n_ang, n_rad, rows, cells, bord...]
    all_to_all x5 -> x0, starting transfers between devices: 20.2 us -> none  [the longest x4 15.9 us: route_reply(): lax.all_to_all(doubled, ('panel', 'ang'), split_axis=1, concat_axis=1, ti...]
    gather x4 -> x0, local copies, waits for them, and re-layouts: 11.6 us -> none  [overset(): jnp.take(table, gather_index, axis=1).reshape(stacked_rows, slot_count, 4)]
    reshape x8 -> x2, local copies, waits for them, and re-layouts: 11.2 us -> 0.17 us  [the longest x1 0.09 us: body(): partner_device.reshape(border, 1)]
    select_n x14 -> x0, other arithmetic: 6.29 us -> none  [the longest x4 4.77 us: evaluate(): lower_r = jnp.where(first_r, mirror * current[:, :1], haloed[:, :1, 1:-1])]
    slice x13 -> x0, local copies, waits for them, and re-layouts: 4.19 us -> none  [the longest x8 3.46 us: padded(): last = lax.slice_in_dim(value, length - width, length, axis=dim)]
  transfers between devices with their start and end apart: 21 -> 0, of which waited for: 10 -> 0; matrix products, arithmetic and copies ran while one was open for 28% -> 0% of each run, Pallas kernels for 0% -> 0%
where the time goes in v1:
time: 49.5 us; the launch traced here: 49.2 us
  Pallas kernels  41.9 us (85%)
  local copies, waits for them, and re-layouts  6.69 us (14%)
  between operations  0.66 us (1%)
    pallas_call x1, Pallas kernels, body(): pl.pallas_call(functools.partial(kernel, (n_ang, n_rad, rows, cells, bord...  41.9 us
    unnamed x19, local copies, waits for them, and re-layouts  6.52 us

profile of v1, /device:TPU:0, one launch (start us, length us, event | category | flops | bytes accessed | tf_op | source)
XLA Modules:
  0.0 49.2 jit_solution(8180120339123692296)
XLA Ops:
  0.6 0.0 copy-start.7
  0.6 0.6 %copy-done.7 = s32[1,32,1]{1,2,0:T(1,128)S(1)} copy-done((s32[1,32,1]{1,2,0:T(1,128)S(1)}, s32[1,32,1]{1,2,0:T(1,128)}, u32[]{:S(2)}) %copy-start.7) | copy-done | bytes 152
  1.3 0.0 copy-start.6
  1.3 0.1 copy.11.pdev
  1.4 0.6 %copy-done.6 = f32[1,32,4]{1,2,0:T(4,128)S(1)} copy-done((f32[1,32,4]{1,2,0:T(4,128)S(1)}, f32[1,32,4]{1,2,0:T(4,128)}, u32[]{:S(2)}) %copy-start.6) | copy-done | bytes 536
  2.0 0.0 copy-start.3
  2.0 0.0 copy-start.4
  2.0 0.0 copy-start.5
  2.0 0.1 copy.12.pweight
  2.1 0.6 %copy-done.3 = s32[1,32]{1,0:T(1,128)S(1)} copy-done((s32[1,32]{1,0:T(1,128)S(1)}, s32[1,32]{1,0:T(1,128)}, u32[]{:S(2)}) %copy-start.3) | copy-done | bytes 152
  2.6 0.0 copy-done.4
  2.6 0.0 copy-done.5
  2.7 0.0 copy-start
  2.7 0.9 %copy-done = f32[1,3,2,16,512]{4,3,2,1,0:T(8,128)S(1)} copy-done((f32[1,3,2,16,512]{4,3,2,1,0:T(8,128)S(1)}, f32[1,3,2,16,512]{4,3,2,1,0:T(8,128)}, u32[]{:S(2)}) %copy-start) | copy-done | bytes 196632
  3.6 0.0 copy-start.1
  3.6 0.9 %copy-done.1 = f32[1,3,2,16,512]{4,3,2,1,0:T(8,128)S(1)} copy-done((f32[1,3,2,16,512]{4,3,2,1,0:T(8,128)S(1)}, f32[1,3,2,16,512]{4,3,2,1,0:T(8,128)}, u32[]{:S(2)}) %copy-start.1) | copy-done | bytes 196632
  4.5 0.0 copy-start.2
  4.5 0.8 %copy-done.2 = f32[1,2,16,512]{3,2,1,0:T(8,128)S(1)} copy-done((f32[1,2,16,512]{3,2,1,0:T(8,128)S(1)}, f32[1,2,16,512]{3,2,1,0:T(8,128)}, u32[]{:S(2)}) %copy-start.2) | copy-done | bytes 65560
  5.4 41.9 %shard_map.103 = (f32[32,512]{1,0:T(8,128)S(1)}, f32[3,32,512]{2,1,0:T(8,128)S(1)}, f32[3,32,512]{2,1,0:T(8,128)S(1)}) custom-call(f32[32,512]{1,0:T(8,128)S(1)} %bitcast.12, f32[3,32,512]{2,1,0:T(8,128)S(1)} %bitcast.8, f32[3,32,512]{2,1,0:T(8,128)S(1)} %bitcast.9, s32[32,1]{1,0:T(8,128)S(1)} %copy.11.pdev, s32[1,32]{1,0:T(1,128)S(1)} %copy-done.3, ...), custom_call_target="tpu_custom_call" | custom-call | tf_op jit(solution)/shard_map/pallas_call | solution.py:547
  47.2 0.6 %copy.16 = f32[1,2,16,512]{3,2,1,0:T(8,128)} copy(f32[1,2,16,512]{3,2,1,0:T(8,128)S(1)} %bitcast.13) | data formatting | bytes 131072
  47.9 0.7 %copy.17 = f32[1,3,2,16,512]{4,3,2,1,0:T(8,128)} copy(f32[1,3,2,16,512]{4,3,2,1,0:T(8,128)S(1)} %bitcast.11) | data formatting | bytes 393216
  48.6 0.7 %copy.18 = f32[1,3,2,16,512]{4,3,2,1,0:T(8,128)} copy(f32[1,3,2,16,512]{4,3,2,1,0:T(8,128)S(1)} %bitcast.10) | data formatting | bytes 393216
Async XLA Ops:
  0.6 0.7 %copy-start.7 = (s32[1,32,1]{1,2,0:T(1,128)S(1)}, s32[1,32,1]{1,2,0:T(1,128)}, u32[]{:S(2)}) copy-start(s32[1,32,1]{1,2,0:T(1,128)} %param.11) | copy-start | bytes 388
  1.3 0.7 %copy-start.6 = (f32[1,32,4]{1,2,0:T(4,128)S(1)}, f32[1,32,4]{1,2,0:T(4,128)}, u32[]{:S(2)}) copy-start(f32[1,32,4]{1,2,0:T(4,128)} %param.14) | copy-start | bytes 1540
  2.0 0.7 %copy-start.3 = (s32[1,32]{1,0:T(1,128)S(1)}, s32[1,32]{1,0:T(1,128)}, u32[]{:S(2)}) copy-start(s32[1,32]{1,0:T(1,128)} %pphi.1) | copy-start | bytes 388
  2.0 0.7 %copy-start.4 = (s32[1,32]{1,0:T(1,128)S(1)}, s32[1,32]{1,0:T(1,128)}, u32[]{:S(2)}) copy-start(s32[1,32]{1,0:T(1,128)} %ptheta.1) | copy-start | bytes 388
  2.0 0.7 %copy-start.5 = (f32[1,32]{1,0:T(1,128)S(1)}, f32[1,32]{1,0:T(1,128)}, u32[]{:S(2)}) copy-start(f32[1,32]{1,0:T(1,128)} %pturn.1) | copy-start | bytes 388
  2.7 0.9 %copy-start = (f32[1,3,2,16,512]{4,3,2,1,0:T(8,128)S(1)}, f32[1,3,2,16,512]{4,3,2,1,0:T(8,128)}, u32[]{:S(2)}) copy-start(f32[1,3,2,16,512]{4,3,2,1,0:T(8,128)} %param.9) | copy-start | bytes 589828
  3.6 0.9 %copy-start.1 = (f32[1,3,2,16,512]{4,3,2,1,0:T(8,128)S(1)}, f32[1,3,2,16,512]{4,3,2,1,0:T(8,128)}, u32[]{:S(2)}) copy-start(f32[1,3,2,16,512]{4,3,2,1,0:T(8,128)} %param.10) | copy-start | bytes 589828
  4.5 0.8 %copy-start.2 = (f32[1,2,16,512]{3,2,1,0:T(8,128)S(1)}, f32[1,2,16,512]{3,2,1,0:T(8,128)}, u32[]{:S(2)}) copy-start(f32[1,2,16,512]{3,2,1,0:T(8,128)} %param.8) | copy-start | bytes 196612

commit v2 on v1

--- a/solution.py
+++ b/solution.py
@@ -15,6 +15,7 @@
 FIELDS = 7
 LANES = 128
 LEVELS = 8
+vmem_bytes = 64 * 1024 * 1024 - 256 * 1024
 ahead = (0.5 * time_step, 0.5 * time_step, time_step)
 share = (time_step / 6.0, time_step / 3.0, time_step / 3.0, time_step / 6.0)
 
@@ -65,12 +66,13 @@
 
 def kernel(
     sizes,
-    den, mom, mag, pdev, pphi, ptheta, pweight, pturn,
+    den, mom, mag, pdev_hbm, pphi_hbm, ptheta_hbm, pweight_hbm, pturn_hbm,
     oden, omom, omag,
+    pdev, pphi, ptheta, pweight, pturn,
     land, staged, state, total, slope, x_low, x_high, geo,
     phi_in, theta_out, theta_in, over_out, over_in,
     meta_out, meta_in, coef, picker,
-    own_sem, load_send, load_recv, give_send, give_recv,
+    small_sem, own_sem, load_send, load_recv, give_send, give_recv,
     meta_send, meta_recv, phi_send, phi_recv, theta_send, theta_recv,
     over_send, over_recv,
 ):
@@ -87,6 +89,16 @@
     def at(panel, ang, rad):
         return {"panel": panel, "ang": ang, "rad": rad}
 
+    small = [
+        pltpu.make_async_copy(src, dst, small_sem.at[i])
+        for i, (src, dst) in enumerate((
+            (pdev_hbm, pdev), (pphi_hbm, pphi), (ptheta_hbm, ptheta),
+            (pweight_hbm, pweight), (pturn_hbm, pturn),
+        ))
+    ]
+    for copy in small:
+        copy.start()
+
     barrier = pltpu.get_barrier_semaphore()
 
     def greet(i, carry):
@@ -139,12 +151,15 @@
         wide = jnp.broadcast_to(row, (border, border))
         return jnp.sum(jnp.where(square, wide, 0.0), axis=1, keepdims=True)
 
-    place = lane_b == sub_b + border * lax.rem(a, per_tile)
+    spot_b = jnp.where(sub_b < side_rows, 2 * sub_b, 2 * sub_b - (border - 1))
+    place = lane_b == spot_b + border * lax.rem(a, per_tile)
+    for copy in small:
+        copy.wait()
     columns = [
-        pdev[...].astype(jnp.float32),
+        column(pdev[...].astype(jnp.float32)),
         column(pphi[...].astype(jnp.float32)),
         column(ptheta[...].astype(jnp.float32)),
-    ] + [pweight[:, i:i + 1] for i in range(4)]
+    ] + [column(pweight[i:i + 1, :]) for i in range(4)]
     meta_out[...] = jnp.zeros_like(meta_out)
     for i, col in enumerate(columns):
         meta_out[i:i + 1, :] = jnp.sum(
@@ -153,8 +168,9 @@
 
     at_low = t == 0
     at_high = t == n_rad - 1
-    base_row = jnp.where(at_high, side_rows, 0)
-    turn_at = sub_b == base_row + lax.rem(lane_b, side_rows)
+    shifted = jnp.where(spot_b % 2 == 0, spot_b, lax.rem(spot_b + LANES - 2, LANES))
+    ghosted = jnp.where(shifted % 2 == 0, at_low.astype(jnp.int32), at_high.astype(jnp.int32))
+    turn_at = (lane_b == shifted) & (ghosted == 1)
     angle = jnp.sum(
         jnp.where(turn_at, jnp.broadcast_to(column(pturn[...]), (border, LANES)), 0.0),
         axis=0, keepdims=True,
@@ -244,19 +260,20 @@
     for copy in loads:
         copy.wait_recv()
 
-    block_of = lane8 // side_rows
+    block_of = lane8 // border
+    pair8 = lane8 // 2
+    even = lane8 % 2 == 0
     first_lane = lane8 == 0
     last_lane = lane8 == LANES - 1
     first_level = sub8 == 0
     last_level = sub8 == LEVELS - 1
 
     def pack(k, f, value, packs):
-        low, high = packs
-        spot = f * cells + k
-        hit = lane8 == spot
-        low = jnp.where(hit, pltpu.roll(value, spot, 1), low)
-        high = jnp.where(hit, pltpu.roll(value, spot + 1, 1), high)
-        return low, high
+        spot = border * (f % per_tile) + 2 * k + 1
+        hit = pair8 == border // 2 * (f % per_tile) + k
+        packs[f // per_tile] = jnp.where(
+            hit, pltpu.roll(value, lax.rem(spot, LANES), 1), packs[f // per_tile]
+        )
 
     def phi_copies(s):
         down = pltpu.make_async_remote_copy(
@@ -275,13 +292,13 @@
 
     def theta_copies(s):
         down = pltpu.make_async_remote_copy(
-            src_ref=theta_out.at[s, 0], dst_ref=theta_in.at[s, 1],
+            src_ref=theta_out.at[s], dst_ref=theta_in.at[s, 1],
             send_sem=theta_send.at[s, 0], recv_sem=theta_recv.at[s, 1],
             device_id=at(mine, a, jnp.maximum(t - 1, 0)),
             device_id_type=pl.DeviceIdType.MESH,
         )
         up = pltpu.make_async_remote_copy(
-            src_ref=theta_out.at[s, 1], dst_ref=theta_in.at[s, 0],
+            src_ref=theta_out.at[s], dst_ref=theta_in.at[s, 0],
             send_sem=theta_send.at[s, 1], recv_sem=theta_recv.at[s, 0],
             device_id=at(mine, a, jnp.minimum(t + 1, n_rad - 1)),
             device_id_type=pl.DeviceIdType.MESH,
@@ -290,14 +307,13 @@
 
     def over_copy(s, q):
         return pltpu.make_async_remote_copy(
-            src_ref=over_out.at[s, q], dst_ref=over_in.at[s, a * n_rad + t],
+            src_ref=over_out.at[s, q // 2], dst_ref=over_in.at[s, a * n_rad + t],
             send_sem=over_send.at[s], recv_sem=over_recv.at[s],
             device_id=at(other, q // 2, lax.rem(q, 2) * (n_rad - 1)),
             device_id_type=pl.DeviceIdType.MESH,
         )
 
-    def send_all(s, packs):
-        theta_out[s, 0], theta_out[s, 1] = packs
+    def send_all(s):
         theta_down, theta_up = theta_copies(s)
         phi_down, phi_up = phi_copies(s)
         for can, copy in (
@@ -307,34 +323,39 @@
             pl.when(can)(copy.start)
 
         def overset(g, carry):
-            turned = []
-            for f in range(FIELDS):
-                value = state[s, :, f].reshape(cells * LEVELS, LANES)
-                head = value.astype(jnp.bfloat16)
-                rest = (value - head.astype(jnp.float32)).astype(jnp.bfloat16)
-                got = jnp.dot(
-                    jnp.concatenate([head, rest], axis=1), picker[g],
-                    preferred_element_type=jnp.float32,
-                )
-                ghost = None
-                for k in range(cells):
-                    piece = got[k * LEVELS:(k + 1) * LEVELS]
-                    term = (
-                        piece[:, :LANES] * coef[g, 0, k:k + 1, :]
-                        + piece[:, LANES:] * coef[g, 1, k:k + 1, :]
-                    )
-                    ghost = term if ghost is None else ghost + term
-                turned.append(pltpu.roll(ghost, f * side_rows, 1) if f else ghost)
-            groups = LANES // side_rows
-            for j in range(groups):
-                message = turned[0]
+            value = state[s].reshape(cells * FIELDS * LEVELS, LANES)
+            head = value.astype(jnp.bfloat16)
+            rest = (value - head.astype(jnp.float32)).astype(jnp.bfloat16)
+            got = jnp.dot(
+                jnp.concatenate([head, rest], axis=1), picker[g],
+                preferred_element_type=jnp.float32,
+            )
+            ghosts = [None] * FIELDS
+            for k in range(cells):
+                near = jnp.broadcast_to(coef[g, 0, k:k + 1, :], (LEVELS, LANES))
+                far = jnp.broadcast_to(coef[g, 1, k:k + 1, :], (LEVELS, LANES))
                 for f in range(FIELDS):
-                    message = jnp.where(block_of == (f + j) % groups, turned[f], message)
-                if j:
-                    message = pltpu.roll(message, LANES - j * side_rows, 1)
-                over_out[s, g * groups + j] = message
-            for j in range(groups):
-                over_copy(s, g * groups + j).start()
+                    at_row = (k * FIELDS + f) * LEVELS
+                    piece = got[at_row:at_row + LEVELS]
+                    term = piece[:, :LANES] * near + piece[:, LANES:] * far
+                    ghosts[f] = term if k == 0 else ghosts[f] + term
+            turned = [
+                pltpu.roll(ghosts[f], border * (f % per_tile), 1) if f % per_tile else ghosts[f]
+                for f in range(FIELDS)
+            ]
+            for j in range(per_tile):
+                for half in range(2):
+                    members = range(half * per_tile, min(FIELDS, (half + 1) * per_tile))
+                    message = turned[members[0]]
+                    for f in members:
+                        message = jnp.where(
+                            block_of == (f + j) % per_tile, turned[f], message
+                        )
+                    if j:
+                        message = pltpu.roll(message, LANES - j * border, 1)
+                    over_out[s, g * per_tile + j, half] = message
+            for j in range(2 * per_tile):
+                over_copy(s, g * 2 * per_tile + j).start()
             return carry
 
         if tiles == 1:
@@ -367,7 +388,7 @@
                 x_high[k + 1, f] = high_p[f]
             return carry
 
-        lax.fori_loop(0, cells, row, 0, unroll=2)
+        lax.fori_loop(0, cells, row, 0, unroll=4)
 
     def halos(s):
         half_t, mix_t, half_p, mix_p, centre = [geo[i] for i in range(5)]
@@ -416,15 +437,6 @@
         def _():
             pltpu.make_async_copy(over_in.at[s], over_in.at[s], over_recv.at[s]).wait()
             ghost = jnp.sum(over_in[s], axis=0)
-            nexts = pltpu.roll(ghost, LANES - side_rows, 1)
-            lasts = pltpu.roll(ghost, side_rows, 1)
-            is_theta = (block_of == 2) | (block_of == 5)
-            is_phi = (block_of == 3) | (block_of == 6)
-            ghost = jnp.where(
-                is_theta, cosine * ghost + sine * nexts,
-                jnp.where(is_phi, cosine * ghost - sine * lasts, ghost),
-            )
-
             @pl.when(at_low)
             def _():
                 theta_in[s, 0] = ghost
@@ -433,60 +445,73 @@
             def _():
                 theta_in[s, 1] = ghost
 
-        lower, upper = theta_in[s, 0], theta_in[s, 1]
-        half_lane = LANES // 2
-        is_low = lane8 < half_lane
+        both = [
+            jnp.where(even, theta_in[s, 0, h], pltpu.roll(theta_in[s, 1, h], LANES - 2, 1))
+            for h in range(2)
+        ]
         u = []
         for f in range(FIELDS):
-            here = pltpu.roll(lower, LANES - f * cells, 1) if f else lower
-            there = pltpu.roll(upper, (half_lane - f * cells) % LANES, 1)
-            u.append(jnp.where(is_low, here, there))
+            away = border * (f % per_tile)
+            value = both[f // per_tile]
+            u.append(pltpu.roll(value, LANES - away, 1) if away else value)
+        for f in (2, 5):
+            u[f], u[f + 1] = cosine * u[f] + sine * u[f + 1], cosine * u[f + 1] - sine * u[f]
         speed, pressure = point_values(u)
-        signed = jnp.where(is_low, half_t, -half_t)
+        signed = jnp.where(even, half_t, -half_t)
         edge, _ = low_high(u, flux_of(u, speed, pressure, 1, {}, {}), signed, mix_t)
         return edge
 
     def tend(k, f, edge):
-        low = pltpu.roll(edge[f], lax.rem(LANES - k, LANES), 1)
-        high = pltpu.roll(edge[f], LANES // 2 - 1 - k, 1)
-        ends = jnp.where(first_lane, low, jnp.where(last_lane, high, 0.0))
+        ends = pltpu.roll(edge[f], lax.rem(LANES - 2 * k, LANES), 1)
+        ends = jnp.where(outer_lanes, ends, 0.0)
         return (slope[k, f] + ends) + (x_low[k, f] + x_high[k + 2, f])
 
     zero8 = jnp.zeros((LEVELS, LANES), jnp.float32)
+    outer_lanes = first_lane | last_lane
 
     def enter(k, packs):
+        packs = list(packs)
         for f in range(FIELDS):
             value = land[f, pl.ds(k, LEVELS, stride=cells), :]
             state[0, k, f] = value
-            packs = pack(k, f, value, packs)
-        return packs
-
-    packs = lax.fori_loop(0, cells, enter, (zero8, zero8), unroll=True)
-
-    for s in range(4):
-        send_all(s, packs)
+            total[k, f] = value
+            pack(k, f, value, packs)
+        return tuple(packs)
+
+    def keep(s, packs):
+        for half in range(2):
+            theta_out[s, half] = packs[half]
+
+    keep(0, lax.fori_loop(0, cells, enter, (zero8, zero8), unroll=4))
+
+    def stage(s, carry):
+        send_all(s)
         inner(s)
         edge = halos(s)
-        if s < 3:
-            def advance(k, packs):
-                for f in range(FIELDS):
-                    base = state[0, k, f]
-                    k_now = tend(k, f, edge)
-                    value = base + ahead[s] * k_now
-                    state[s + 1, k, f] = value
-                    packs = pack(k, f, value, packs)
-                    total[k, f] = (base if s == 0 else total[k, f]) + share[s] * k_now
-                return packs
-
-            packs = lax.fori_loop(0, cells, advance, (zero8, zero8), unroll=True)
-        else:
-            def finish(k, carry):
-                for f in range(FIELDS):
-                    value = total[k, f] + share[s] * tend(k, f, edge)
-                    staged[f, pl.ds(k, LEVELS, stride=cells), :] = value
-                return carry
-
-            lax.fori_loop(0, cells, finish, 0, unroll=True)
+        step_on = jnp.where(s < 2, ahead[0], ahead[2])
+        weight = jnp.where((s == 0) | (s == 3), share[0], share[1])
+
+        def advance(k, packs):
+            packs = list(packs)
+            for f in range(FIELDS):
+                now = tend(k, f, edge)
+                value = state[0, k, f] + step_on * now
+                state[s + 1, k, f] = value
+                pack(k, f, value, packs)
+                total[k, f] = total[k, f] + weight * now
+            return tuple(packs)
+
+        keep(s + 1, lax.fori_loop(0, cells, advance, (zero8, zero8), unroll=4))
+        return carry
+
+    lax.fori_loop(0, 4, stage, 0)
+
+    def leave(k, carry):
+        for f in range(FIELDS):
+            staged[f, pl.ds(k, LEVELS, stride=cells), :] = total[k, f]
+        return carry
+
+    lax.fori_loop(0, cells, leave, 0, unroll=4)
 
     gives = []
     for step in range(1, n_rad):
@@ -523,10 +548,26 @@
             (a > 0, phi_down), (a < n_ang - 1, phi_up),
         ):
             pl.when(can)(copy.wait_send)
-        pltpu.make_async_copy(over_out.at[s], over_out.at[s], over_send.at[s]).wait()
+        for _ in range(2):
+            pltpu.make_async_copy(over_out.at[s], over_out.at[s], over_send.at[s]).wait()
     for copy in keeps:
         copy.wait()
     for copy in gives:
+        copy.wait()
+
+
+def hand_over(one, two, three, out_one, out_two, out_three, sems):
+    copies = [
+        pltpu.make_async_copy(src, dst, sems.at[i])
+        for i, (src, dst) in enumerate(
+            [(one, out_one)]
+            + [(two.at[c], out_two.at[c]) for c in range(3)]
+            + [(three.at[c], out_three.at[c]) for c in range(3)]
+        )
+    ]
+    for copy in copies:
+        copy.start()
+    for copy in copies:
         copy.wait()
 
 
@@ -537,13 +578,13 @@
     n_ang, n_rad = lax.axis_size("ang"), lax.axis_size("rad")
     rows = rows_r * cells
     assert rows_r * n_rad == LEVELS and n_theta == LANES * n_rad and n_rad > 1
-    assert LANES % border == 0 and n_ang % (LANES // border) == 0 and border == 2 * cells
+    assert border * 4 == LANES and n_ang % (LANES // border) == 0 and border == 2 * cells
     f32 = jnp.float32
     tiles = n_ang * border // LANES
     sources = n_ang * n_rad
     vmem = pltpu.VMEM
     dma = pltpu.SemaphoreType.DMA
-    spaces = [pl.BlockSpec(memory_space=pl.ANY)] * 3 + [pl.BlockSpec(memory_space=vmem)] * 5
+    spaces = [pl.BlockSpec(memory_space=pltpu.HBM)] * 8
     outs = pl.pallas_call(
         functools.partial(kernel, (n_ang, n_rad, rows, cells, border)),
         out_shape=(
@@ -554,38 +595,48 @@
         in_specs=spaces,
         out_specs=[pl.BlockSpec(memory_space=pl.ANY)] * 3,
         scratch_shapes=[
+            vmem((1, border), jnp.int32), vmem((1, border), jnp.int32),
+            vmem((1, border), jnp.int32), vmem((4, border), f32), vmem((1, border), f32),
             vmem((FIELDS, LEVELS * cells, LANES), f32),
             vmem((FIELDS, LEVELS * cells, LANES), f32),
-            vmem((4, cells, FIELDS, LEVELS, LANES), f32),
+            vmem((5, cells, FIELDS, LEVELS, LANES), f32),
             vmem((cells, FIELDS, LEVELS, LANES), f32),
             vmem((cells, FIELDS, LEVELS, LANES), f32),
             vmem((cells + 2, FIELDS, LEVELS, LANES), f32),
             vmem((cells + 2, FIELDS, LEVELS, LANES), f32),
             vmem((5, LEVELS, LANES), f32),
             vmem((4, 2, FIELDS, LEVELS, LANES), f32),
-            vmem((4, 2, LEVELS, LANES), f32),
-            vmem((4, 2, LEVELS, LANES), f32),
-            vmem((4, 2 * n_ang, LEVELS, LANES), f32),
-            vmem((4, sources, LEVELS, LANES), f32),
+            vmem((5, 2, LEVELS, LANES), f32),
+            vmem((4, 2, 2, LEVELS, LANES), f32),
+            vmem((4, n_ang, 2, LEVELS, LANES), f32),
+            vmem((4, sources, 2, LEVELS, LANES), f32),
             vmem((LEVELS, LANES), f32),
             vmem((n_ang, LEVELS, LANES), f32),
             vmem((tiles, 2, cells, LANES), f32),
             vmem((tiles, 2 * LANES, 2 * LANES), jnp.bfloat16),
-            dma((3,)), dma((3, n_rad)), dma((3, n_rad)), dma((3, n_rad)), dma((3, n_rad)),
+            dma((5,)), dma((3,)), dma((3, n_rad)), dma((3, n_rad)), dma((3, n_rad)), dma((3, n_rad)),
             dma, dma, dma((4, 2)), dma((4, 2)), dma((4, 2)), dma((4, 2)), dma((4,)), dma((4,)),
         ],
         compiler_params=pltpu.CompilerParams(
-            collective_id=0, has_side_effects=True, vmem_limit_bytes=32 * 1024 * 1024
+            collective_id=0, has_side_effects=True, vmem_limit_bytes=vmem_bytes
         ),
     )(
         density.reshape(rows, n_theta),
         momentum.reshape(3, rows, n_theta),
         magnetic.reshape(3, rows, n_theta),
-        partner_device.reshape(border, 1),
+        partner_device.reshape(1, border),
         partner_phi, partner_theta,
-        partner_weight.reshape(border, 4),
+        partner_weight.reshape(border, 4).T,
         border_turn,
     )
+    outs = pl.pallas_call(
+        hand_over,
+        out_shape=tuple(jax.ShapeDtypeStruct(o.shape, f32) for o in outs),
+        in_specs=[pl.BlockSpec(memory_space=pl.ANY)] * 3,
+        out_specs=[pl.BlockSpec(memory_space=pltpu.HBM)] * 3,
+        scratch_shapes=[dma((FIELDS,))],
+        compiler_params=pltpu.CompilerParams(vmem_limit_bytes=vmem_bytes),
+    )(*outs)
     return (
         outs[0].reshape(density.shape),
         outs[1].reshape(momentum.shape),

time: 49.5 us -> 61.9 us (1.25)
  Pallas kernels: 41.9 us -> 61.1 us
  local copies, waits for them, and re-layouts: 6.69 us -> 0 us
    pallas_call x0 -> x1, Pallas kernels: none -> 15.1 us  [body(): pl.pallas_call(hand_over, out_shape=tuple((jax.ShapeDtypeStruct(o.shape,...]
    unnamed x19 -> x0, local copies, waits for them, and re-layouts: 6.52 us -> none
    pallas_call x1, Pallas kernels: 41.9 us -> 46.1 us  [body(): pl.pallas_call(functools.partial(kernel, (n_ang, n_rad, rows, cells, bord...]
where the time goes in v2:
time: 61.9 us; the launch traced here: 61.8 us
  Pallas kernels  61.1 us (99%)
  between operations  0.64 us (1%)
    pallas_call x1, Pallas kernels, body(): pl.pallas_call(functools.partial(kernel, (n_ang, n_rad, rows, cells, bord...  46.1 us
    pallas_call x1, Pallas kernels, body(): pl.pallas_call(hand_over, out_shape=tuple((jax.ShapeDtypeStruct(o.shape,...  15.1 us

profile of v2, /device:TPU:0, one launch (start us, length us, event | category | flops | bytes accessed | tf_op | source)
XLA Modules:
  0.0 61.8 jit_solution(6653420401150053950)
XLA Ops:
  0.6 46.1 %shard_map.103 = (f32[32,512]{1,0:T(8,128)}, f32[3,32,512]{2,1,0:T(8,128)}, f32[3,32,512]{2,1,0:T(8,128)}) custom-call(f32[32,512]{1,0:T(8,128)} %bitcast.12, f32[3,32,512]{2,1,0:T(8,128)} %bitcast.10, f32[3,32,512]{2,1,0:T(8,128)} %bitcast.11, s32[1,32]{1,0:T(1,128)} %bitcast.14, s32[1,32]{1,0:T(1,128)} %pphi_hbm.1, s32[1,32]{1,0:T(1,128)} %ptheta_hbm.1, ...), custom_call_target="tpu_custom_call" | custom-call | tf_op jit(solution)/shard_map/pallas_call | solution.py:588
  46.7 15.1 %shard_map.104 = (f32[32,512]{1,0:T(8,128)}, f32[3,32,512]{2,1,0:T(8,128)}, f32[3,32,512]{2,1,0:T(8,128)}) custom-call(f32[32,512]{1,0:T(8,128)} %get-tuple-element.9.one, f32[3,32,512]{2,1,0:T(8,128)} %get-tuple-element.10.two, f32[3,32,512]{2,1,0:T(8,128)} %get-tuple-element.11.three), custom_call_target="tpu_custom_call" | custom-call | tf_op jit(solution)/shard_map/pallas_call | solution.py:632

commit v3 on v2

--- a/solution.py
+++ b/solution.py
@@ -15,7 +15,7 @@
 FIELDS = 7
 LANES = 128
 LEVELS = 8
-vmem_bytes = 64 * 1024 * 1024 - 256 * 1024
+vmem_bytes = 32 * 1024 * 1024
 ahead = (0.5 * time_step, 0.5 * time_step, time_step)
 share = (time_step / 6.0, time_step / 3.0, time_step / 3.0, time_step / 6.0)
 
@@ -68,7 +68,7 @@
     sizes,
     den, mom, mag, pdev_hbm, pphi_hbm, ptheta_hbm, pweight_hbm, pturn_hbm,
     oden, omom, omag,
-    pdev, pphi, ptheta, pweight, pturn,
+    pdev, pphi, ptheta, pweight, pturn, first, fetch_sem,
     land, staged, state, total, slope, x_low, x_high, geo,
     phi_in, theta_out, theta_in, over_out, over_in,
     meta_out, meta_in, coef, picker,
@@ -98,6 +98,13 @@
     ]
     for copy in small:
         copy.start()
+    fetches = [
+        pltpu.make_async_copy(den, first.at[0], fetch_sem.at[0]),
+        pltpu.make_async_copy(mom, first.at[pl.ds(1, 3)], fetch_sem.at[1]),
+        pltpu.make_async_copy(mag, first.at[pl.ds(4, 3)], fetch_sem.at[2]),
+    ]
+    for copy in fetches:
+        copy.start()
 
     barrier = pltpu.get_barrier_semaphore()
 
@@ -197,14 +204,16 @@
         sources + n_rad - 1 + jnp.where(a > 0, 1, 0) + jnp.where(a < n_ang - 1, 1, 0),
     )
 
+    for copy in fetches:
+        copy.wait()
     loads = []
     for step in range(1, n_rad):
         to = lax.rem(t + step, n_rad)
         lanes = pl.ds(pl.multiple_of(to * LANES, LANES), LANES)
         for i, (src, dst) in enumerate((
-            (den.at[:, lanes], land.at[0, own_rows, :]),
-            (mom.at[:, :, lanes], land.at[pl.ds(1, 3), own_rows, :]),
-            (mag.at[:, :, lanes], land.at[pl.ds(4, 3), own_rows, :]),
+            (first.at[0, :, lanes], land.at[0, own_rows, :]),
+            (first.at[pl.ds(1, 3), :, lanes], land.at[pl.ds(1, 3), own_rows, :]),
+            (first.at[pl.ds(4, 3), :, lanes], land.at[pl.ds(4, 3), own_rows, :]),
         )):
             loads.append(pltpu.make_async_remote_copy(
                 src_ref=src, dst_ref=dst,
@@ -597,6 +606,7 @@
         scratch_shapes=[
             vmem((1, border), jnp.int32), vmem((1, border), jnp.int32),
             vmem((1, border), jnp.int32), vmem((4, border), f32), vmem((1, border), f32),
+            vmem((FIELDS, rows, n_theta), f32), dma((3,)),
             vmem((FIELDS, LEVELS * cells, LANES), f32),
             vmem((FIELDS, LEVELS * cells, LANES), f32),
             vmem((5, cells, FIELDS, LEVELS, LANES), f32),
@@ -621,6 +631,7 @@
             collective_id=0, has_side_effects=True, vmem_limit_bytes=vmem_bytes
         ),
     )(
+        *[pltpu.with_memory_space_constraint(x, pltpu.HBM) for x in (
         density.reshape(rows, n_theta),
         momentum.reshape(3, rows, n_theta),
         magnetic.reshape(3, rows, n_theta),
@@ -628,6 +639,7 @@
         partner_phi, partner_theta,
         partner_weight.reshape(border, 4).T,
         border_turn,
+        )]
     )
     outs = pl.pallas_call(
         hand_over,

time: 61.9 us -> 47.4 us (0.77)
  Pallas kernels: 61.1 us -> 46.6 us
    pallas_call x1, Pallas kernels: 15.1 us -> 0.82 us  [body(): pl.pallas_call(hand_over, out_shape=tuple((jax.ShapeDtypeStruct(o.shape,...]
where the time goes in v3:
time: 47.4 us; the launch traced here: 47.2 us
  Pallas kernels  46.6 us (98%)
  between operations  0.64 us (1%)
    pallas_call x1, Pallas kernels, body(): pl.pallas_call(functools.partial(kernel, (n_ang, n_rad, rows, cells, bord...  45.8 us

profile of v3, /device:TPU:0, one launch (start us, length us, event | category | flops | bytes accessed | tf_op | source)
XLA Modules:
  0.0 47.2 jit_solution(16347517519273514147)
XLA Ops:
  0.6 45.8 %shard_map.103 = (f32[32,512]{1,0:T(8,128)S(1)}, f32[3,32,512]{2,1,0:T(8,128)S(1)}, f32[3,32,512]{2,1,0:T(8,128)S(1)}) custom-call(f32[32,512]{1,0:T(8,128)} %bitcast.12, f32[3,32,512]{2,1,0:T(8,128)} %bitcast.10, f32[3,32,512]{2,1,0:T(8,128)} %bitcast.11, s32[1,32]{1,0:T(1,128)} %bitcast.14, s32[1,32]{1,0:T(1,128)} %pphi_hbm.1, s32[1,32]{1,0:T(1,128)} %ptheta_hbm.1, ...), custom_call_target="tpu_custom_call" | custom-call | tf_op jit(solution)/shard_map/pallas_call | solution.py:597
  46.4 0.8 %shard_map.104 = (f32[32,512]{1,0:T(8,128)}, f32[3,32,512]{2,1,0:T(8,128)}, f32[3,32,512]{2,1,0:T(8,128)}) custom-call(f32[32,512]{1,0:T(8,128)S(1)} %get-tuple-element.9.one, f32[3,32,512]{2,1,0:T(8,128)S(1)} %get-tuple-element.10.two, f32[3,32,512]{2,1,0:T(8,128)S(1)} %get-tuple-element.11.three), custom_call_target="tpu_custom_call" | custom-call | tf_op jit(solution)/shard_map/pallas_call | solution.py:644

commit v4 on v3

--- a/solution.py
+++ b/solution.py
@@ -316,7 +316,7 @@
 
     def over_copy(s, q):
         return pltpu.make_async_remote_copy(
-            src_ref=over_out.at[s, q // 2], dst_ref=over_in.at[s, a * n_rad + t],
+            src_ref=over_out.at[s, q], dst_ref=over_in.at[s, a * n_rad + t],
             send_sem=over_send.at[s], recv_sem=over_recv.at[s],
             device_id=at(other, q // 2, lax.rem(q, 2) * (n_rad - 1)),
             device_id_type=pl.DeviceIdType.MESH,
@@ -353,6 +353,7 @@
                 for f in range(FIELDS)
             ]
             for j in range(per_tile):
+                pair = []
                 for half in range(2):
                     members = range(half * per_tile, min(FIELDS, (half + 1) * per_tile))
                     message = turned[members[0]]
@@ -362,7 +363,12 @@
                         )
                     if j:
                         message = pltpu.roll(message, LANES - j * border, 1)
-                    over_out[s, g * per_tile + j, half] = message
+                    pair.append(message)
+                at_pair = 2 * (g * per_tile + j)
+                over_out[s, at_pair] = jnp.where(even, pair[0], pltpu.roll(pair[1], 1, 1))
+                over_out[s, at_pair + 1] = jnp.where(
+                    even, pltpu.roll(pair[0], LANES - 1, 1), pair[1]
+                )
             for j in range(2 * per_tile):
                 over_copy(s, g * 2 * per_tile + j).start()
             return carry
@@ -397,7 +403,7 @@
                 x_high[k + 1, f] = high_p[f]
             return carry
 
-        lax.fori_loop(0, cells, row, 0, unroll=4)
+        lax.fori_loop(0, cells, row, 0, unroll=8)
 
     def halos(s):
         half_t, mix_t, half_p, mix_p, centre = [geo[i] for i in range(5)]
@@ -448,11 +454,13 @@
             ghost = jnp.sum(over_in[s], axis=0)
             @pl.when(at_low)
             def _():
-                theta_in[s, 0] = ghost
+                theta_in[s, 0, 0] = ghost
+                theta_in[s, 0, 1] = pltpu.roll(ghost, LANES - 1, 1)
 
             @pl.when(at_high)
             def _():
-                theta_in[s, 1] = ghost
+                theta_in[s, 1, 0] = pltpu.roll(ghost, 1, 1)
+                theta_in[s, 1, 1] = ghost
 
         both = [
             jnp.where(even, theta_in[s, 0, h], pltpu.roll(theta_in[s, 1, h], LANES - 2, 1))
@@ -491,7 +499,7 @@
         for half in range(2):
             theta_out[s, half] = packs[half]
 
-    keep(0, lax.fori_loop(0, cells, enter, (zero8, zero8), unroll=4))
+    keep(0, lax.fori_loop(0, cells, enter, (zero8, zero8), unroll=True))
 
     def stage(s, carry):
         send_all(s)
@@ -510,7 +518,7 @@
                 total[k, f] = total[k, f] + weight * now
             return tuple(packs)
 
-        keep(s + 1, lax.fori_loop(0, cells, advance, (zero8, zero8), unroll=4))
+        keep(s + 1, lax.fori_loop(0, cells, advance, (zero8, zero8), unroll=True))
         return carry
 
     lax.fori_loop(0, 4, stage, 0)
@@ -557,8 +565,7 @@
             (a > 0, phi_down), (a < n_ang - 1, phi_up),
         ):
             pl.when(can)(copy.wait_send)
-        for _ in range(2):
-            pltpu.make_async_copy(over_out.at[s], over_out.at[s], over_send.at[s]).wait()
+        pltpu.make_async_copy(over_out.at[s], over_out.at[s], over_send.at[s]).wait()
     for copy in keeps:
         copy.wait()
     for copy in gives:
@@ -618,8 +625,8 @@
             vmem((4, 2, FIELDS, LEVELS, LANES), f32),
             vmem((5, 2, LEVELS, LANES), f32),
             vmem((4, 2, 2, LEVELS, LANES), f32),
-            vmem((4, n_ang, 2, LEVELS, LANES), f32),
-            vmem((4, sources, 2, LEVELS, LANES), f32),
+            vmem((4, 2 * n_ang, LEVELS, LANES), f32),
+            vmem((4, sources, LEVELS, LANES), f32),
             vmem((LEVELS, LANES), f32),
             vmem((n_ang, LEVELS, LANES), f32),
             vmem((tiles, 2, cells, LANES), f32),

time: 47.4 us -> 45 us (0.949)
  Pallas kernels: 46.6 us -> 44.2 us
    pallas_call x1, Pallas kernels: 45.8 us -> 43.4 us  [body(): pl.pallas_call(functools.partial(kernel, (n_ang, n_rad, rows, cells, bord...]
where the time goes in v4:
time: 45 us; the launch traced here: 44.9 us
  Pallas kernels  44.2 us (98%)
  between operations  0.64 us (1%)
    pallas_call x1, Pallas kernels, body(): pl.pallas_call(functools.partial(kernel, (n_ang, n_rad, rows, cells, bord...  43.4 us

profile of v4, /device:TPU:0, one launch (start us, length us, event | category | flops | bytes accessed | tf_op | source)
XLA Modules:
  0.0 44.9 jit_solution(6656394925304696721)
XLA Ops:
  0.6 43.4 %shard_map.103 = (f32[32,512]{1,0:T(8,128)S(1)}, f32[3,32,512]{2,1,0:T(8,128)S(1)}, f32[3,32,512]{2,1,0:T(8,128)S(1)}) custom-call(f32[32,512]{1,0:T(8,128)} %bitcast.12, f32[3,32,512]{2,1,0:T(8,128)} %bitcast.10, f32[3,32,512]{2,1,0:T(8,128)} %bitcast.11, s32[1,32]{1,0:T(1,128)} %bitcast.14, s32[1,32]{1,0:T(1,128)} %pphi_hbm.1, s32[1,32]{1,0:T(1,128)} %ptheta_hbm.1, ...), custom_call_target="tpu_custom_call" | custom-call | tf_op jit(solution)/shard_map/pallas_call | solution.py:604
  44.0 0.8 %shard_map.104 = (f32[32,512]{1,0:T(8,128)}, f32[3,32,512]{2,1,0:T(8,128)}, f32[3,32,512]{2,1,0:T(8,128)}) custom-call(f32[32,512]{1,0:T(8,128)S(1)} %get-tuple-element.9.one, f32[3,32,512]{2,1,0:T(8,128)S(1)} %get-tuple-element.10.two, f32[3,32,512]{2,1,0:T(8,128)S(1)} %get-tuple-element.11.three), custom_call_target="tpu_custom_call" | custom-call | tf_op jit(solution)/shard_map/pallas_call | solution.py:651

commit v5 on v4

--- a/solution.py
+++ b/solution.py
@@ -403,7 +403,7 @@
                 x_high[k + 1, f] = high_p[f]
             return carry
 
-        lax.fori_loop(0, cells, row, 0, unroll=8)
+        lax.fori_loop(0, cells, row, 0, unroll=True)
 
     def halos(s):
         half_t, mix_t, half_p, mix_p, centre = [geo[i] for i in range(5)]
@@ -523,12 +523,13 @@
 
     lax.fori_loop(0, 4, stage, 0)
 
-    def leave(k, carry):
-        for f in range(FIELDS):
-            staged[f, pl.ds(k, LEVELS, stride=cells), :] = total[k, f]
-        return carry
-
-    lax.fori_loop(0, cells, leave, 0, unroll=4)
+    def leave(fields):
+        def move(k, carry):
+            for f in fields:
+                staged[f, pl.ds(k, LEVELS, stride=cells), :] = total[k, f]
+            return carry
+
+        lax.fori_loop(0, cells, move, 0, unroll=True)
 
     gives = []
     for step in range(1, n_rad):
@@ -544,8 +545,10 @@
                 send_sem=give_send.at[i, step], recv_sem=give_recv.at[i, step],
                 device_id=at(mine, a, to), device_id_type=pl.DeviceIdType.MESH,
             ))
-    for copy in gives:
-        copy.start()
+    for i, fields in enumerate(((0,), (1, 2, 3), (4, 5, 6))):
+        leave(fields)
+        for copy in gives[i::3]:
+            copy.start()
     keeps = [
         pltpu.make_async_copy(staged.at[0, own_rows, :], oden.at[:, own_lanes], own_sem.at[0]),
         pltpu.make_async_copy(staged.at[pl.ds(1, 3), own_rows, :], omom.at[:, :, own_lanes], own_sem.at[1]),

time: 45 us -> 46.2 us (1.027)
  Pallas kernels: 44.2 us -> 45.4 us
    pallas_call x1, Pallas kernels: 43.4 us -> 44.6 us  [body(): pl.pallas_call(functools.partial(kernel, (n_ang, n_rad, rows, cells, bord...]
where the time goes in v5:
time: 46.2 us; the launch traced here: 46 us
  Pallas kernels  45.4 us (98%)
  between operations  0.64 us (1%)
    pallas_call x1, Pallas kernels, body(): pl.pallas_call(functools.partial(kernel, (n_ang, n_rad, rows, cells, bord...  44.6 us

profile of v5, /device:TPU:0, one launch (start us, length us, event | category | flops | bytes accessed | tf_op | source)
XLA Modules:
  0.0 46.0 jit_solution(3126486282480866191)
XLA Ops:
  0.6 44.6 %shard_map.103 = (f32[32,512]{1,0:T(8,128)S(1)}, f32[3,32,512]{2,1,0:T(8,128)S(1)}, f32[3,32,512]{2,1,0:T(8,128)S(1)}) custom-call(f32[32,512]{1,0:T(8,128)} %bitcast.12, f32[3,32,512]{2,1,0:T(8,128)} %bitcast.10, f32[3,32,512]{2,1,0:T(8,128)} %bitcast.11, s32[1,32]{1,0:T(1,128)} %bitcast.14, s32[1,32]{1,0:T(1,128)} %pphi_hbm.1, s32[1,32]{1,0:T(1,128)} %ptheta_hbm.1, ...), custom_call_target="tpu_custom_call" | custom-call | tf_op jit(solution)/shard_map/pallas_call | solution.py:607
  45.2 0.8 %shard_map.104 = (f32[32,512]{1,0:T(8,128)}, f32[3,32,512]{2,1,0:T(8,128)}, f32[3,32,512]{2,1,0:T(8,128)}) custom-call(f32[32,512]{1,0:T(8,128)S(1)} %get-tuple-element.9.one, f32[3,32,512]{2,1,0:T(8,128)S(1)} %get-tuple-element.10.two, f32[3,32,512]{2,1,0:T(8,128)S(1)} %get-tuple-element.11.three), custom_call_target="tpu_custom_call" | custom-call | tf_op jit(solution)/shard_map/pallas_call | solution.py:654
